TPU v7x, 32 devices: a whole 2x2x4 slice. The times are simulated.
32 devices in a mesh: row: 8 (over z, y), col: 4 (over x, core).
Axes of the slice: x: 2, y: 2, z: 4, core: 2. Of those that a mesh axis runs over, the one named last changes fastest.
Arguments:
- rhs: float32 [32, 65536], P(None, ('row', 'col')), may hold values from -5 to 7
- coords: float32 [3, 65536], P(None, ('row', 'col')), may hold values from 0 to 8, as said below
- nugget: float32 [65536], P(('row', 'col')), may hold values from 1.5 to 3
- near_ids: int32 [128, 3], P(('row', 'col')), may hold values from -1 to 127, as said below
- basis: float32 [7, 128, 65536], P(None, None, ('row', 'col')), may hold values from -6 to 6
Outputs:
- solution: float32 [32, 65536], P(None, ('row', 'col'))
- residual: float32 [32, 65536], P(None, ('row', 'col'))
Inputs may be any that keep to these rules, and one draw needn't show every extreme that they name: `near_ids`: row i lists leaf i and some of the leaves i - 1 to i + 1 inside the range, each at most once, in any order; the other slots hold -1; the first and last leaf of each device's block of 4 list all such leaves inside the range. `coords`: each leaf's points lie in a unit box with an integer corner; consecutive leaves lie in boxes that share a face.
All inputs are finite; a program needn't handle non-finite values.
Results may differ from a plain program's by a relative error of at most 0.0003.
Values sent between devices are 32-bit elements; how exact they have to be, the bound alone decides.
No kernel may reach another device: no remote copies, remote signals or barrier semaphores. Data moves between devices by JAX's collectives and lax.ppermute only.
A program may use at most 128 MiB of HBM per device.

v0:
```python
import jax
import jax.numpy as jnp
from jax import lax
from jax.sharding import PartitionSpec as P

LEAF = 512
ITERS = 4
REACH = 1
WIN = 3


root_three = 1.7320508075688772
spacing_factor = 1.6


def padded(cells, sides, width):
    for axis, dim in sides:
        count = lax.axis_size(axis)
        ends = count - 1
        head = lax.slice_in_dim(cells, 0, width, axis=dim)
        tail = lax.slice_in_dim(cells, cells.shape[dim] - width, cells.shape[dim], axis=dim)
        cells = jnp.concatenate(
            [
                lax.ppermute(tail, axis, [(i, (i + 1) % count) for i in range(ends)]),
                cells,
                lax.ppermute(head, axis, [((i + 1) % count, i) for i in range(ends)]),
            ],
            axis=dim,
        )
    return cells


def partner(value, axis, stride):
    mask = 2**stride
    pairs = [(source, source ^ mask) for source in range(lax.axis_size(axis))]
    return lax.ppermute(value, axis, pairs)


def matern(square_dist):
    length = spacing_factor * LEAF ** (-1.0 / 3.0)
    scaled = root_three * jnp.sqrt(square_dist) / length
    return (1.0 + scaled) * jnp.exp(-scaled)


def window_mask(near_ids, first_leaf, count):
    leaves = first_leaf + jnp.arange(count, dtype=jnp.int32)
    offsets = jnp.arange(WIN, dtype=jnp.int32) - REACH
    target = leaves[None, :] + offsets[:, None]
    matches = near_ids.T[None, :, :] == target[:, None, :]
    return jnp.any(matches, axis=1).astype(jnp.float32)


def tile_block(own_coords, far_coords, weight):
    spread = own_coords[:, :, :, None] - far_coords[:, :, None, :]
    square_dist = jnp.sum(spread * spread, axis=0)
    return matern(square_dist) * (weight / (16 * WIN))[:, None, None]


def per_device(rhs, coords, nugget, near_ids, basis):
    width = rhs.shape[1]
    leaves = width // LEAF
    levels = basis.shape[0]
    leaf_bits = leaves.bit_length() - 1
    col_bits = lax.axis_size("col").bit_length() - 1
    mask = window_mask(near_ids, lax.axis_index(("row", "col")) * leaves, leaves)
    coord_halo = padded(coords, ((("row", "col"), 1),), REACH * LEAF)
    own = coords.reshape(3, leaves, LEAF)

    def build_tiles():
        return [
            tile_block(
                own,
                coord_halo[:, offset * LEAF : offset * LEAF + width].reshape(3, leaves, LEAF),
                mask[offset],
            )
            for offset in range(WIN)
        ]

    def near_field(field):
        tile_list = build_tiles()
        field_halo = padded(field, ((("row", "col"), 1),), REACH * LEAF)
        total = jnp.zeros(field.shape, jnp.float32)
        for offset in range(WIN):
            segment = field_halo[:, offset * LEAF : offset * LEAF + width].reshape(-1, leaves, LEAF)
            part_sum = jnp.einsum(
                "bij,rbj->rbi", tile_list[offset], segment, precision=lax.Precision.HIGHEST
            )
            total = total + part_sum.reshape(-1, width)
        return total

    def combine_levels(partials):
        count = len(partials)
        summed = []
        for index in range(count):
            total = partials[index]
            span_bits = index + 1
            for bit_pos in range(min(span_bits, col_bits)):
                total = total + partner(total, "col", bit_pos)
            for bit_pos in range(span_bits - col_bits):
                total = total + partner(total, "row", bit_pos)
            summed.append(total)
        return summed

    def far_field(field):
        total = jnp.zeros(field.shape, jnp.float32)
        partials = []
        for level in range(levels):
            cluster = LEAF * 2 ** (level + 1)
            if level + 1 - leaf_bits <= 0:
                grouped = basis[level].reshape(-1, width // cluster, cluster)
                values = field.reshape(-1, width // cluster, cluster)
                skeleton = jnp.einsum(
                    "kcs,rcs->crk", grouped, values, precision=lax.Precision.HIGHEST
                )
                spread_back = jnp.einsum(
                    "kcs,crk->rcs", grouped, skeleton, precision=lax.Precision.HIGHEST
                )
                total = total + spread_back.reshape(-1, width) / cluster
            else:
                partials.append(
                    jnp.einsum("kp,rp->rk", basis[level], field, precision=lax.Precision.HIGHEST)
                )
        summed = combine_levels(partials)
        for index in range(len(summed)):
            level = leaf_bits + index
            cluster = LEAF * 2 ** (level + 1)
            spread_back = jnp.einsum(
                "kp,rk->rp", basis[level], summed[index], precision=lax.Precision.HIGHEST
            )
            total = total + spread_back / cluster
        return total

    def operate(field):
        return nugget[None, :] * field + near_field(field) + far_field(field)

    def squares(values):
        return lax.psum(jnp.sum(values * values, axis=1), ("row", "col"))

    def iteration(step, carry):
        solution, residual, direction, norm_now = carry
        image = operate(direction)
        step_size = norm_now / lax.psum(jnp.sum(direction * image, axis=1), ("row", "col"))
        solution = solution + step_size[:, None] * direction
        residual = residual - step_size[:, None] * image
        norm_next = squares(residual)
        direction = residual + (norm_next / norm_now)[:, None] * direction
        return (solution, residual, direction, norm_next)

    start_state = (jnp.zeros(rhs.shape, jnp.float32), rhs, rhs, squares(rhs))
    solution, residual, direction, norm_now = lax.fori_loop(0, ITERS, iteration, start_state)
    return (solution, residual)


def solution(mesh):
    placed = (
        P(None, ("row", "col")),
        P(None, ("row", "col")),
        P(("row", "col")),
        P(("row", "col"), None),
        P(None, None, ("row", "col")),
    )
    return jax.shard_map(
        per_device,
        mesh=mesh,
        in_specs=placed,
        out_specs=(P(None, ("row", "col")), P(None, ("row", "col"))),
        check_vma=False,
    )
```

profile of v0, /device:TPU:0, one launch (start us, length us, event | category | flops | bytes accessed | tf_op | source)
XLA Modules:
  0.0 690.0 jit_solution(6137361765909497343)
XLA Ops:
  7.0 44.7 %psum.29 = f32[32]{0:T(128)S(1)} all-reduce(f32[32]{0:T(128)S(1)} %multiply_reduce_fusion.5), channel_id=1, replica_groups=mesh['row'=8,'col'=4] {'row','col'}, use_global_device_ids=true, to_apply=%region_1.0 | all-reduce | flops 32 | bytes 256 | tf_op jit(solution)/shard_map/psum | solution.py:137
  52.5 8.6 %copy.26 = f32[7,128,2048]{1,2,0:T(8,128)} copy(f32[7,128,2048]{2,1,0:T(8,128)} %param.11) | data formatting | bytes 14680064
  61.1 628.1 %while.21 = (s32[]{:T(128)}, f32[32,2048]{1,0:T(8,128)S(1)}, f32[32,2048]{1,0:T(8,128)S(1)}, f32[32,2048]{1,0:T(8,128)S(1)}, f32[32]{0:T(128)S(1)}, /*index=5*/f...) while((s32[]{:T(128)}, f32[32,2048]{1,0:T(8,128)S(1)}, ...), condition=%wide.wide.region_11.0_spmd.clone, body=%wide.wide.region_3.0_spmd.clone.sunk | while | flops 2660233216 | bytes 90311792 | solution.py:150
  78.7 9.6 %multiply_reduce_fusion.12 = (f32[4,512,512]{2,1,0:T(8,128)}, f32[4,512,512]{2,1,0:T(8,128)}, f32[4,512,512]{2,1,0:T(8,128)}) fusion(f32[3,4,512]{2,1,0:T(4,128)S(1)} %sub.131, f32[3,4,512]{2,1,0:T(4,128)S(1)} %get-tuple-element.447, f32[3,4,512]{2,1,0:T(4,128)S(1)} %sub.132), kind=kLoop, calls=%fused_computation.clone.clone.1 | loop fusion | flops 25165824 | bytes 12656640 | tf_op jit(solution)/shard_map/while/body/eval_jaxpr/reduce_sum | solution.py:55
  112.8 7.6 %fusion.257 = f32[32,4,512]{2,0,1:T(8,128)S(1)} fusion(f32[4,512,512]{2,1,0:T(8,128)} %get-tuple-element.395, f32[4]{0:T(128)S(1)} %get-tuple-element.396, f32[4,4,8,512]{3,2,1,0:T(8,128)S(1)} %bitcast.209), kind=kOutput, calls=%fused_computation.49.clone.clone.1 | convolution fusion | flops 407896064 | bytes 4718608 | tf_op jit(solution)/shard_map/while/body/eval_jaxpr/bij,rbj->rbi/dot_general | solution.py:85
  120.4 5.8 fusion.258
  126.2 5.4 fusion.259
  138.9 39.3 %psum.36 = f32[32]{0:T(128)S(1)} all-reduce(f32[32]{0:T(128)S(1)} %get-tuple-element.406), channel_id=1, replica_groups=mesh['row'=8,'col'=4] {'row','col'}, use_global_device_ids=true, to_apply=%region_8.0 | all-reduce | flops 32 | bytes 256 | tf_op jit(solution)/shard_map/while/body/eval_jaxpr/psum | solution.py:142
  178.4 40.2 %psum.37 = f32[32]{0:T(128)S(1)} all-reduce(f32[32]{0:T(128)S(1)} %get-tuple-element.408), channel_id=1, replica_groups=mesh['row'=8,'col'=4] {'row','col'}, use_global_device_ids=true, to_apply=%region_10.0 | all-reduce | flops 32 | bytes 256 | tf_op jit(solution)/shard_map/while/body/eval_jaxpr/psum | solution.py:137
  236.4 9.6 %multiply_reduce_fusion.12 = (f32[4,512,512]{2,1,0:T(8,128)}, f32[4,512,512]{2,1,0:T(8,128)}, f32[4,512,512]{2,1,0:T(8,128)}) fusion(f32[3,4,512]{2,1,0:T(4,128)S(1)} %sub.131, f32[3,4,512]{2,1,0:T(4,128)S(1)} %get-tuple-element.447, f32[3,4,512]{2,1,0:T(4,128)S(1)} %sub.132), kind=kLoop, calls=%fused_computation.clone.clone.1 | loop fusion | flops 25165824 | bytes 12656640 | tf_op jit(solution)/shard_map/while/body/eval_jaxpr/reduce_sum | solution.py:55
  269.4 7.6 %fusion.257 = f32[32,4,512]{2,0,1:T(8,128)S(1)} fusion(f32[4,512,512]{2,1,0:T(8,128)} %get-tuple-element.395, f32[4]{0:T(128)S(1)} %get-tuple-element.396, f32[4,4,8,512]{3,2,1,0:T(8,128)S(1)} %bitcast.209), kind=kOutput, calls=%fused_computation.49.clone.clone.1 | convolution fusion | flops 407896064 | bytes 4718608 | tf_op jit(solution)/shard_map/while/body/eval_jaxpr/bij,rbj->rbi/dot_general | solution.py:85
  277.0 5.8 fusion.258
  295.5 39.2 %psum.36 = f32[32]{0:T(128)S(1)} all-reduce(f32[32]{0:T(128)S(1)} %get-tuple-element.406), channel_id=1, replica_groups=mesh['row'=8,'col'=4] {'row','col'}, use_global_device_ids=true, to_apply=%region_8.0 | all-reduce | flops 32 | bytes 256 | tf_op jit(solution)/shard_map/while/body/eval_jaxpr/psum | solution.py:142
  335.0 40.2 %psum.37 = f32[32]{0:T(128)S(1)} all-reduce(f32[32]{0:T(128)S(1)} %get-tuple-element.408), channel_id=1, replica_groups=mesh['row'=8,'col'=4] {'row','col'}, use_global_device_ids=true, to_apply=%region_10.0 | all-reduce | flops 32 | bytes 256 | tf_op jit(solution)/shard_map/while/body/eval_jaxpr/psum | solution.py:137
  393.0 9.6 %multiply_reduce_fusion.12 = (f32[4,512,512]{2,1,0:T(8,128)}, f32[4,512,512]{2,1,0:T(8,128)}, f32[4,512,512]{2,1,0:T(8,128)}) fusion(f32[3,4,512]{2,1,0:T(4,128)S(1)} %sub.131, f32[3,4,512]{2,1,0:T(4,128)S(1)} %get-tuple-element.447, f32[3,4,512]{2,1,0:T(4,128)S(1)} %sub.132), kind=kLoop, calls=%fused_computation.clone.clone.1 | loop fusion | flops 25165824 | bytes 12656640 | tf_op jit(solution)/shard_map/while/body/eval_jaxpr/reduce_sum | solution.py:55
  426.6 7.6 %fusion.257 = f32[32,4,512]{2,0,1:T(8,128)S(1)} fusion(f32[4,512,512]{2,1,0:T(8,128)} %get-tuple-element.395, f32[4]{0:T(128)S(1)} %get-tuple-element.396, f32[4,4,8,512]{3,2,1,0:T(8,128)S(1)} %bitcast.209), kind=kOutput, calls=%fused_computation.49.clone.clone.1 | convolution fusion | flops 407896064 | bytes 4718608 | tf_op jit(solution)/shard_map/while/body/eval_jaxpr/bij,rbj->rbi/dot_general | solution.py:85
  434.2 5.8 fusion.258
  452.7 39.3 %psum.36 = f32[32]{0:T(128)S(1)} all-reduce(f32[32]{0:T(128)S(1)} %get-tuple-element.406), channel_id=1, replica_groups=mesh['row'=8,'col'=4] {'row','col'}, use_global_device_ids=true, to_apply=%region_8.0 | all-reduce | flops 32 | bytes 256 | tf_op jit(solution)/shard_map/while/body/eval_jaxpr/psum | solution.py:142
  492.2 40.2 %psum.37 = f32[32]{0:T(128)S(1)} all-reduce(f32[32]{0:T(128)S(1)} %get-tuple-element.408), channel_id=1, replica_groups=mesh['row'=8,'col'=4] {'row','col'}, use_global_device_ids=true, to_apply=%region_10.0 | all-reduce | flops 32 | bytes 256 | tf_op jit(solution)/shard_map/while/body/eval_jaxpr/psum | solution.py:137
  550.2 9.6 %multiply_reduce_fusion.12 = (f32[4,512,512]{2,1,0:T(8,128)}, f32[4,512,512]{2,1,0:T(8,128)}, f32[4,512,512]{2,1,0:T(8,128)}) fusion(f32[3,4,512]{2,1,0:T(4,128)S(1)} %sub.131, f32[3,4,512]{2,1,0:T(4,128)S(1)} %get-tuple-element.447, f32[3,4,512]{2,1,0:T(4,128)S(1)} %sub.132), kind=kLoop, calls=%fused_computation.clone.clone.1 | loop fusion | flops 25165824 | bytes 12656640 | tf_op jit(solution)/shard_map/while/body/eval_jaxpr/reduce_sum | solution.py:55
  583.3 7.6 %fusion.257 = f32[32,4,512]{2,0,1:T(8,128)S(1)} fusion(f32[4,512,512]{2,1,0:T(8,128)} %get-tuple-element.395, f32[4]{0:T(128)S(1)} %get-tuple-element.396, f32[4,4,8,512]{3,2,1,0:T(8,128)S(1)} %bitcast.209), kind=kOutput, calls=%fused_computation.49.clone.clone.1 | convolution fusion | flops 407896064 | bytes 4718608 | tf_op jit(solution)/shard_map/while/body/eval_jaxpr/bij,rbj->rbi/dot_general | solution.py:85
  590.9 5.8 fusion.258
  609.3 39.2 %psum.36 = f32[32]{0:T(128)S(1)} all-reduce(f32[32]{0:T(128)S(1)} %get-tuple-element.406), channel_id=1, replica_groups=mesh['row'=8,'col'=4] {'row','col'}, use_global_device_ids=true, to_apply=%region_8.0 | all-reduce | flops 32 | bytes 256 | tf_op jit(solution)/shard_map/while/body/eval_jaxpr/psum | solution.py:142
  648.8 40.2 %psum.37 = f32[32]{0:T(128)S(1)} all-reduce(f32[32]{0:T(128)S(1)} %get-tuple-element.408), channel_id=1, replica_groups=mesh['row'=8,'col'=4] {'row','col'}, use_global_device_ids=true, to_apply=%region_10.0 | all-reduce | flops 32 | bytes 256 | tf_op jit(solution)/shard_map/while/body/eval_jaxpr/psum | solution.py:137
  (332 shorter events, 219.7 us)
Async XLA Ops:
  2.3 58.8 %collective-permute-start.17 = (f32[3,512]{1,0:T(4,128)S(1)}, f32[3,512]{1,0:T(4,128)S(1)}, u32[]{:S(2)}, u32[]{:S(2)}) collective-permute-start(f32[3,512]{1,0:T(4,128)S(1)} %get-tuple-element.248), channel_id=1, source_target_pairs={{0,1},{1,2},{2,3},{3,4},{4,5},{5,6},{6,7},{7,8},{8,9},{9,10},{10,1... | collective-permute-start | bytes 18440 | tf_op jit(solution)/shard_map/ppermute | solution.py:24
  4.7 56.4 %collective-permute-start.18 = (f32[3,512]{1,0:T(4,128)S(1)}, f32[3,512]{1,0:T(4,128)S(1)}, u32[]{:S(2)}, u32[]{:S(2)}) collective-permute-start(f32[3,512]{1,0:T(4,128)S(1)} %get-tuple-element.249), channel_id=1, source_target_pairs={{1,0},{2,1},{3,2},{4,3},{5,4},{6,5},{7,6},{8,7},{9,8},{10,9},{11,1... | collective-permute-start | bytes 18440 | tf_op jit(solution)/shard_map/ppermute | solution.py:26
  63.0 27.2 %collective-permute-start.5 = (f32[32,128]{1,0:T(8,128)S(1)}, f32[32,128]{1,0:T(8,128)S(1)}, u32[]{:S(2)}, u32[]{:S(2)}) collective-permute-start(f32[32,128]{1,0:T(8,128)S(1)} %fusion.247), channel_id=1, source_target_pairs={{0,1},{1,0},{2,3},{3,2},{4,5},{5,4},{6,7},{7,6},{8,9},{9,8},{10,11... | collective-permute-start | bytes 49160 | tf_op jit(solution)/shard_map/while/body/eval_jaxpr/ppermute | solution.py:36
  65.0 28.2 %collective-permute-start.9 = (f32[32,128]{1,0:T(8,128)S(1)}, f32[32,128]{1,0:T(8,128)S(1)}, u32[]{:S(2)}, u32[]{:S(2)}) collective-permute-start(f32[32,128]{1,0:T(8,128)S(1)} %fusion.248), channel_id=1, source_target_pairs={{0,1},{1,0},{2,3},{3,2},{4,5},{5,4},{6,7},{7,6},{8,9},{9,8},{10,11... | collective-permute-start | bytes 49160 | tf_op jit(solution)/shard_map/while/body/eval_jaxpr/ppermute | solution.py:36
  69.4 26.0 %collective-permute-start.12 = (f32[32,128]{1,0:T(8,128)S(1)}, f32[32,128]{1,0:T(8,128)S(1)}, u32[]{:S(2)}, u32[]{:S(2)}) collective-permute-start(f32[32,128]{1,0:T(8,128)S(1)} %fusion.249), channel_id=1, source_target_pairs={{0,1},{1,0},{2,3},{3,2},{4,5},{5,4},{6,7},{7,6},{8,9},{9,8},{10,11... | collective-permute-start | bytes 49160 | tf_op jit(solution)/shard_map/while/body/eval_jaxpr/ppermute | solution.py:36
  70.0 42.8 %collective-permute-start.15 = (f32[32,512]{1,0:T(8,128)S(1)}, f32[32,512]{1,0:T(8,128)S(1)}, u32[]{:S(2)}, u32[]{:S(2)}) collective-permute-start(f32[32,512]{1,0:T(8,128)S(1)} %get-tuple-element.397), channel_id=1, source_target_pairs={{1,0},{2,1},{3,2},{4,3},{5,4},{6,5},{7,6},{8,7},{9,8},{10,9},{11,1... | collective-permute-start | bytes 196616 | tf_op jit(solution)/shard_map/while/body/eval_jaxpr/ppermute | solution.py:26
  105.1 31.3 %collective-permute-start.14 = (f32[32,128]{1,0:T(8,128)S(1)}, f32[32,128]{1,0:T(8,128)S(1)}, u32[]{:S(2)}, u32[]{:S(2)}) collective-permute-start(f32[32,128]{1,0:T(8,128)S(1)} %fusion.254), channel_id=1, source_target_pairs={{0,1},{1,0},{2,3},{3,2},{4,5},{5,4},{6,7},{7,6},{8,9},{9,8},{10,11... | collective-permute-start | bytes 49160 | tf_op jit(solution)/shard_map/while/body/eval_jaxpr/ppermute | solution.py:36
  105.2 26.4 %collective-permute-start.8 = (f32[32,128]{1,0:T(8,128)S(1)}, f32[32,128]{1,0:T(8,128)S(1)}, u32[]{:S(2)}, u32[]{:S(2)}) collective-permute-start(f32[32,128]{1,0:T(8,128)S(1)} %add.450), channel_id=1, source_target_pairs={{0,8},{4,12},{8,0},{12,4},{16,24},{20,28},{24,16},{28,20},{1,9},{5... | collective-permute-start | bytes 49160 | tf_op jit(solution)/shard_map/while/body/eval_jaxpr/ppermute | solution.py:36
  220.7 27.2 %collective-permute-start.5 = (f32[32,128]{1,0:T(8,128)S(1)}, f32[32,128]{1,0:T(8,128)S(1)}, u32[]{:S(2)}, u32[]{:S(2)}) collective-permute-start(f32[32,128]{1,0:T(8,128)S(1)} %fusion.247), channel_id=1, source_target_pairs={{0,1},{1,0},{2,3},{3,2},{4,5},{5,4},{6,7},{7,6},{8,9},{9,8},{10,11... | collective-permute-start | bytes 49160 | tf_op jit(solution)/shard_map/while/body/eval_jaxpr/ppermute | solution.py:36
  222.6 28.2 %collective-permute-start.9 = (f32[32,128]{1,0:T(8,128)S(1)}, f32[32,128]{1,0:T(8,128)S(1)}, u32[]{:S(2)}, u32[]{:S(2)}) collective-permute-start(f32[32,128]{1,0:T(8,128)S(1)} %fusion.248), channel_id=1, source_target_pairs={{0,1},{1,0},{2,3},{3,2},{4,5},{5,4},{6,7},{7,6},{8,9},{9,8},{10,11... | collective-permute-start | bytes 49160 | tf_op jit(solution)/shard_map/while/body/eval_jaxpr/ppermute | solution.py:36
  227.0 26.0 %collective-permute-start.12 = (f32[32,128]{1,0:T(8,128)S(1)}, f32[32,128]{1,0:T(8,128)S(1)}, u32[]{:S(2)}, u32[]{:S(2)}) collective-permute-start(f32[32,128]{1,0:T(8,128)S(1)} %fusion.249), channel_id=1, source_target_pairs={{0,1},{1,0},{2,3},{3,2},{4,5},{5,4},{6,7},{7,6},{8,9},{9,8},{10,11... | collective-permute-start | bytes 49160 | tf_op jit(solution)/shard_map/while/body/eval_jaxpr/ppermute | solution.py:36
  227.6 41.8 %collective-permute-start.15 = (f32[32,512]{1,0:T(8,128)S(1)}, f32[32,512]{1,0:T(8,128)S(1)}, u32[]{:S(2)}, u32[]{:S(2)}) collective-permute-start(f32[32,512]{1,0:T(8,128)S(1)} %get-tuple-element.397), channel_id=1, source_target_pairs={{1,0},{2,1},{3,2},{4,3},{5,4},{6,5},{7,6},{8,7},{9,8},{10,9},{11,1... | collective-permute-start | bytes 196616 | tf_op jit(solution)/shard_map/while/body/eval_jaxpr/ppermute | solution.py:26
  262.8 30.3 %collective-permute-start.14 = (f32[32,128]{1,0:T(8,128)S(1)}, f32[32,128]{1,0:T(8,128)S(1)}, u32[]{:S(2)}, u32[]{:S(2)}) collective-permute-start(f32[32,128]{1,0:T(8,128)S(1)} %fusion.254), channel_id=1, source_target_pairs={{0,1},{1,0},{2,3},{3,2},{4,5},{5,4},{6,7},{7,6},{8,9},{9,8},{10,11... | collective-permute-start | bytes 49160 | tf_op jit(solution)/shard_map/while/body/eval_jaxpr/ppermute | solution.py:36
  377.3 27.2 %collective-permute-start.5 = (f32[32,128]{1,0:T(8,128)S(1)}, f32[32,128]{1,0:T(8,128)S(1)}, u32[]{:S(2)}, u32[]{:S(2)}) collective-permute-start(f32[32,128]{1,0:T(8,128)S(1)} %fusion.247), channel_id=1, source_target_pairs={{0,1},{1,0},{2,3},{3,2},{4,5},{5,4},{6,7},{7,6},{8,9},{9,8},{10,11... | collective-permute-start | bytes 49160 | tf_op jit(solution)/shard_map/while/body/eval_jaxpr/ppermute | solution.py:36
  379.2 28.2 %collective-permute-start.9 = (f32[32,128]{1,0:T(8,128)S(1)}, f32[32,128]{1,0:T(8,128)S(1)}, u32[]{:S(2)}, u32[]{:S(2)}) collective-permute-start(f32[32,128]{1,0:T(8,128)S(1)} %fusion.248), channel_id=1, source_target_pairs={{0,1},{1,0},{2,3},{3,2},{4,5},{5,4},{6,7},{7,6},{8,9},{9,8},{10,11... | collective-permute-start | bytes 49160 | tf_op jit(solution)/shard_map/while/body/eval_jaxpr/ppermute | solution.py:36
  383.6 26.0 %collective-permute-start.12 = (f32[32,128]{1,0:T(8,128)S(1)}, f32[32,128]{1,0:T(8,128)S(1)}, u32[]{:S(2)}, u32[]{:S(2)}) collective-permute-start(f32[32,128]{1,0:T(8,128)S(1)} %fusion.249), channel_id=1, source_target_pairs={{0,1},{1,0},{2,3},{3,2},{4,5},{5,4},{6,7},{7,6},{8,9},{9,8},{10,11... | collective-permute-start | bytes 49160 | tf_op jit(solution)/shard_map/while/body/eval_jaxpr/ppermute | solution.py:36
  384.2 42.4 %collective-permute-start.15 = (f32[32,512]{1,0:T(8,128)S(1)}, f32[32,512]{1,0:T(8,128)S(1)}, u32[]{:S(2)}, u32[]{:S(2)}) collective-permute-start(f32[32,512]{1,0:T(8,128)S(1)} %get-tuple-element.397), channel_id=1, source_target_pairs={{1,0},{2,1},{3,2},{4,3},{5,4},{6,5},{7,6},{8,7},{9,8},{10,9},{11,1... | collective-permute-start | bytes 196616 | tf_op jit(solution)/shard_map/while/body/eval_jaxpr/ppermute | solution.py:26
  419.3 30.8 %collective-permute-start.14 = (f32[32,128]{1,0:T(8,128)S(1)}, f32[32,128]{1,0:T(8,128)S(1)}, u32[]{:S(2)}, u32[]{:S(2)}) collective-permute-start(f32[32,128]{1,0:T(8,128)S(1)} %fusion.254), channel_id=1, source_target_pairs={{0,1},{1,0},{2,3},{3,2},{4,5},{5,4},{6,7},{7,6},{8,9},{9,8},{10,11... | collective-permute-start | bytes 49160 | tf_op jit(solution)/shard_map/while/body/eval_jaxpr/ppermute | solution.py:36
  419.5 26.0 %collective-permute-start.8 = (f32[32,128]{1,0:T(8,128)S(1)}, f32[32,128]{1,0:T(8,128)S(1)}, u32[]{:S(2)}, u32[]{:S(2)}) collective-permute-start(f32[32,128]{1,0:T(8,128)S(1)} %add.450), channel_id=1, source_target_pairs={{0,8},{4,12},{8,0},{12,4},{16,24},{20,28},{24,16},{28,20},{1,9},{5... | collective-permute-start | bytes 49160 | tf_op jit(solution)/shard_map/while/body/eval_jaxpr/ppermute | solution.py:36
  534.5 27.2 %collective-permute-start.5 = (f32[32,128]{1,0:T(8,128)S(1)}, f32[32,128]{1,0:T(8,128)S(1)}, u32[]{:S(2)}, u32[]{:S(2)}) collective-permute-start(f32[32,128]{1,0:T(8,128)S(1)} %fusion.247), channel_id=1, source_target_pairs={{0,1},{1,0},{2,3},{3,2},{4,5},{5,4},{6,7},{7,6},{8,9},{9,8},{10,11... | collective-permute-start | bytes 49160 | tf_op jit(solution)/shard_map/while/body/eval_jaxpr/ppermute | solution.py:36
  536.4 28.2 %collective-permute-start.9 = (f32[32,128]{1,0:T(8,128)S(1)}, f32[32,128]{1,0:T(8,128)S(1)}, u32[]{:S(2)}, u32[]{:S(2)}) collective-permute-start(f32[32,128]{1,0:T(8,128)S(1)} %fusion.248), channel_id=1, source_target_pairs={{0,1},{1,0},{2,3},{3,2},{4,5},{5,4},{6,7},{7,6},{8,9},{9,8},{10,11... | collective-permute-start | bytes 49160 | tf_op jit(solution)/shard_map/while/body/eval_jaxpr/ppermute | solution.py:36
  540.9 26.0 %collective-permute-start.12 = (f32[32,128]{1,0:T(8,128)S(1)}, f32[32,128]{1,0:T(8,128)S(1)}, u32[]{:S(2)}, u32[]{:S(2)}) collective-permute-start(f32[32,128]{1,0:T(8,128)S(1)} %fusion.249), channel_id=1, source_target_pairs={{0,1},{1,0},{2,3},{3,2},{4,5},{5,4},{6,7},{7,6},{8,9},{9,8},{10,11... | collective-permute-start | bytes 49160 | tf_op jit(solution)/shard_map/while/body/eval_jaxpr/ppermute | solution.py:36
  541.4 41.8 %collective-permute-start.15 = (f32[32,512]{1,0:T(8,128)S(1)}, f32[32,512]{1,0:T(8,128)S(1)}, u32[]{:S(2)}, u32[]{:S(2)}) collective-permute-start(f32[32,512]{1,0:T(8,128)S(1)} %get-tuple-element.397), channel_id=1, source_target_pairs={{1,0},{2,1},{3,2},{4,3},{5,4},{6,5},{7,6},{8,7},{9,8},{10,9},{11,1... | collective-permute-start | bytes 196616 | tf_op jit(solution)/shard_map/while/body/eval_jaxpr/ppermute | solution.py:26
  576.6 30.3 %collective-permute-start.14 = (f32[32,128]{1,0:T(8,128)S(1)}, f32[32,128]{1,0:T(8,128)S(1)}, u32[]{:S(2)}, u32[]{:S(2)}) collective-permute-start(f32[32,128]{1,0:T(8,128)S(1)} %fusion.254), channel_id=1, source_target_pairs={{0,1},{1,0},{2,3},{3,2},{4,5},{5,4},{6,7},{7,6},{8,9},{9,8},{10,11... | collective-permute-start | bytes 49160 | tf_op jit(solution)/shard_map/while/body/eval_jaxpr/ppermute | solution.py:36
  (58 other events, 571.2 us)
where the time goes:
time: 693 us; the launch traced here: 690 us
  blocking collectives  362 us (52%)
  matrix products  184 us (27%)
  starting transfers between devices  79.1 us (11%)
  other arithmetic  40.5 us (6%)
  local copies, waits for them, and re-layouts  18.3 us (3%)
    psum x5, blocking collectives, squares(): return lax.psum(jnp.sum(values * values, axis=1), ('row', 'col'))  205 us
    psum x4, blocking collectives, iteration(): lax.psum(jnp.sum(direction * image, axis=1), ('row', 'col'))  157 us
    dot_general x12, matrix products, near_field(): jnp.einsum('bij,rbj->rbi', tile_list[offset], segment, precision=lax.Prec...  75 us
    ppermute x60, starting transfers between devices, partner(): return lax.ppermute(value, axis, pairs)  63.9 us
    dot_general x20, matrix products, far_field(): jnp.einsum('kp,rk->rp', basis[level], summed[index], precision=lax.Precis...  47.7 us
    reduce_sum x4, other arithmetic, tile_block(): square_dist = jnp.sum(spread * spread, axis=0)  38.3 us
    dot_general x20, matrix products, far_field(): jnp.einsum('kp,rp->rk', basis[level], field, precision=lax.Precision.HIGH...  37.5 us
    dot_general x8, matrix products, far_field(): jnp.einsum('kcs,crk->rcs', grouped, skeleton, precision=lax.Precision.HIG...  14 us
  transfers between devices with their start and end apart: 70, of which 4 were waited for; matrix products, arithmetic and copies ran while one was open for 32% of the time, Pallas kernels for 0%

commit v1 on v0

v1 whole, which is shorter than its diff:
```python
import functools

import jax
import jax.numpy as jnp
from jax import lax
from jax.experimental import pallas as pl
from jax.experimental.pallas import tpu as pltpu
from jax.sharding import PartitionSpec as P

LEAF = 512
ITERS = 4
REACH = 1
WIN = 3
LANES = 128
LOCAL = 3
CHUNK = 64

root_three = 1.7320508075688772
spacing_factor = 1.6
matern_scale = root_three / (spacing_factor * LEAF ** (-1.0 / 3.0))

BOTH = ("row", "col")
ROWS_COLS = (((1,), (0,)), ((), ()))
ROWS_ROWS = (((1,), (1,)), ((), ()))


def halves(values):
    high = values.astype(jnp.bfloat16)
    low = (values - high.astype(jnp.float32)).astype(jnp.bfloat16)
    return high, low


def stacked(values):
    return jnp.concatenate(halves(values), axis=0)


def product(stack, high, low, dims):
    rows = stack.shape[0] // 2
    main = lax.dot_general(stack, high, dims, preferred_element_type=jnp.float32)
    rest = lax.dot_general(stack[:rows], low, dims, preferred_element_type=jnp.float32)
    return main[:rows] + (main[rows:] + rest)


def row_sum(values):
    return jnp.sum(values, axis=1, keepdims=True)


def in_lanes(columns, shape):
    lane = lax.broadcasted_iota(jnp.int32, shape, 1)
    block = jnp.zeros(shape, jnp.float32)
    for index, column in enumerate(columns):
        block = jnp.where(lane == index, column, block)
    return block


def whole(memory=pltpu.VMEM):
    return pl.BlockSpec(memory_space=memory)


def call(body, outs, *args, specs=None, flops=0, limit=32, **extra):
    return pl.pallas_call(
        body,
        out_shape=outs,
        in_specs=specs or [whole()] * len(args),
        out_specs=[whole()] * len(outs),
        compiler_params=pltpu.CompilerParams(vmem_limit_bytes=limit * 2**20),
        cost_estimate=pl.CostEstimate(flops=flops, bytes_accessed=2**20, transcendentals=0),
        **extra,
    )(*args)


def f32(*shape):
    return jax.ShapeDtypeStruct(shape, jnp.float32)


def bf16(*shape):
    return jax.ShapeDtypeStruct(shape, jnp.bfloat16)


def split_kernel(basis_ref, high_ref, low_ref):
    high_ref[...], low_ref[...] = halves(basis_ref[0])


def split_basis(basis):
    levels, rank, width = basis.shape
    return pl.pallas_call(
        split_kernel,
        out_shape=[bf16(levels * rank, width)] * 2,
        grid=(levels,),
        in_specs=[pl.BlockSpec((1, rank, width), lambda level: (level, 0, 0))],
        out_specs=[pl.BlockSpec((rank, width), lambda level: (level, 0))] * 2,
        compiler_params=pltpu.CompilerParams(vmem_limit_bytes=16 * 2**20),
    )(basis)


def kernel_matrices(lane_ref, sub_ref, high_ref, low_ref):
    leaves = lane_ref.shape[1] // LEAF - 2
    parts = LEAF // CHUNK

    def one(step, carry):
        matrix = step // parts
        part = step % parts
        pair = matrix >= leaves
        row_leaf = jnp.where(pair, matrix - leaves, matrix + 1)
        col_leaf = jnp.where(pair, matrix - leaves + 1, matrix + 1)
        row_at = pl.multiple_of(row_leaf * LEAF + part * CHUNK, CHUNK)
        col_at = pl.multiple_of(col_leaf * LEAF, LEAF)
        square = None
        for axis in range(3):
            spread = sub_ref[pl.ds(row_at, CHUNK), axis : axis + 1] - lane_ref[axis : axis + 1, pl.ds(col_at, LEAF)]
            square = spread * spread if square is None else square + spread * spread
        square = square * (matern_scale * matern_scale)
        scaled = square * lax.rsqrt(jnp.maximum(square, 1e-30))
        values = (1.0 + scaled) * jnp.exp(-scaled)
        out_at = pl.ds(pl.multiple_of(part * CHUNK, CHUNK), CHUNK)
        high_ref[matrix, out_at], low_ref[matrix, out_at] = halves(values)
        return carry

    lax.fori_loop(0, (2 * leaves + 1) * parts, one, 0)


def down_kernel(field_ref, high_ref, low_ref, out_ref):
    rank = LANES
    half = field_ref.shape[1] // 2
    stack = stacked(field_ref[...])
    for part in range(2):
        points = slice(part * half, (part + 1) * half)
        out_ref[:, part * rank : (part + 1) * rank] = product(
            stack[:, points], high_ref[:rank, points], low_ref[:rank, points], ROWS_ROWS
        )
    out_ref[:, 2 * rank :] = product(stack, high_ref[rank:], low_ref[rank:], ROWS_ROWS)


def near_kernel(first, *refs):
    (place_ref, ids_ref, field_ref, before_ref, after_ref, nugget_ref, high_ref, low_ref, skel_ref) = refs[:9]
    if first:
        out_ref, message_ref = refs[9:]
    else:
        direction_ref, image_ref, old_skel_ref, out_ref, message_ref = refs[9:]
    rows, width = field_ref.shape
    leaves = width // LEAF

    def weight(leaf, offset):
        target = place_ref[0] * leaves + leaf + offset
        found = ids_ref[leaf, 0] == target
        for slot in range(1, WIN):
            found = jnp.logical_or(found, ids_ref[leaf, slot] == target)
        return jnp.where(found, 1.0 / (16 * WIN), 0.0)

    def own(ref, leaf):
        return ref[:, leaf * LEAF : (leaf + 1) * LEAF]

    pieces = [stacked(before_ref[...])] + [stacked(own(field_ref, leaf)) for leaf in range(leaves)]
    pieces = pieces + [stacked(after_ref[...])]
    square = with_image = cross = 0.0
    for leaf in range(leaves):
        field = own(field_ref, leaf)
        before = product(pieces[leaf], high_ref[leaves + leaf], low_ref[leaves + leaf], ROWS_COLS)
        inside = product(pieces[leaf + 1], high_ref[leaf], low_ref[leaf], ROWS_COLS)
        after = product(pieces[leaf + 2], high_ref[leaves + leaf + 1], low_ref[leaves + leaf + 1], ROWS_ROWS)
        total = own(nugget_ref, leaf) * field + weight(leaf, 0) * inside
        total = total + weight(leaf, -1) * before + weight(leaf, 1) * after
        out_ref[:, leaf * LEAF : (leaf + 1) * LEAF] = total
        square = square + row_sum(field * field)
        with_image = with_image + row_sum(field * total)
        if not first:
            cross = cross + row_sum(field * own(image_ref, leaf) + own(direction_ref, leaf) * total)
    for block in range(LOCAL):
        scale = 1.0 / (LEAF * (2 if block < 2 else 4))
        here = slice(block * LANES, (block + 1) * LANES)
        with_image = with_image + scale * row_sum(skel_ref[:, here] * skel_ref[:, here])
        if not first:
            cross = cross + scale * row_sum(skel_ref[:, here] * old_skel_ref[:, here])
    wide = message_ref.shape[1] - LANES
    message_ref[:, :wide] = skel_ref[:, LOCAL * LANES :]
    message_ref[:, wide:] = in_lanes([square, with_image, cross], (rows, LANES))


def combine_kernel(first, cluster, *refs):
    if first:
        mine_ref, other_ref, next_ref, level_ref = refs
    else:
        mine_ref, other_ref, old_ref, next_ref, level_ref = refs
    total = mine_ref[...] + other_ref[...]
    level = total[:, :LANES]
    level_ref[...] = level
    columns = [0.0, row_sum(level * level) * (1.0 / cluster)]
    if not first:
        columns.append(row_sum(level * old_ref[...]) * (1.0 / cluster))
    wide = total.shape[1] - 2 * LANES
    if wide:
        next_ref[:, :wide] = total[:, LANES : LANES + wide]
    next_ref[:, wide:] = total[:, LANES + wide :] + in_lanes(columns, level.shape)


def up_kernel(first, last, crossing, *refs):
    refs = list(refs)
    high_ref, low_ref, near_ref, field_ref, sums_ref, skel_ref = refs[:6]
    level_refs = refs[6 : 6 + crossing]
    refs = refs[6 + crossing :]
    if not first:
        solution_ref, direction_ref, image_ref, old_skel_ref, state_ref = refs[:5]
        refs = refs[5:]
    if last:
        new_solution_ref, new_field_ref = refs
    else:
        (
            new_solution_ref,
            new_field_ref,
            new_direction_ref,
            new_image_ref,
            new_skel_ref,
            new_state_ref,
            head_ref,
            tail_ref,
        ) = refs
    rows, width = field_ref.shape
    half = width // 2
    norm = sums_ref[:, 0:1]
    curve = sums_ref[:, 1:2]
    if not first:
        ratio = norm / state_ref[:, 0:1]
        curve = curve + ratio * (sums_ref[:, 2:3] + ratio * state_ref[:, 1:2])
    step = norm / curve
    blocks = [skel_ref[:, block * LANES : (block + 1) * LANES] for block in range(LOCAL)]
    blocks = blocks + [ref[...] for ref in level_refs]
    scaled = [block * (1.0 / (LEAF * (2 ** max(index, 1)))) for index, block in enumerate(blocks)]
    for part in range(2):
        points = slice(part * half, (part + 1) * half)
        stack = stacked(jnp.concatenate([scaled[part]] + scaled[2:], axis=1))
        image = near_ref[:, points] + product(stack, high_ref[:, points], low_ref[:, points], ROWS_COLS)
        direction = field_ref[:, points]
        if not first:
            image = image + ratio * image_ref[:, points]
            direction = direction + ratio * direction_ref[:, points]
        moved = step * direction
        new_solution_ref[:, points] = moved if first else solution_ref[:, points] + moved
        new_field_ref[:, points] = field_ref[:, points] - step * image
        if not last:
            new_direction_ref[:, points] = direction
            new_image_ref[:, points] = image
    if not last:
        head_ref[...] = new_field_ref[:, :LEAF]
        tail_ref[...] = new_field_ref[:, width - LEAF :]
        for index, block in enumerate(blocks):
            here = slice(index * LANES, (index + 1) * LANES)
            new_skel_ref[:, here] = block if first else block + ratio * old_skel_ref[:, here]
        new_state_ref[...] = in_lanes([norm, curve], (rows, LANES))


def per_device(rhs, coords, nugget, near_ids, basis):
    rows, width = rhs.shape
    levels, rank, _ = basis.shape
    leaves = width // LEAF
    crossing = levels - (leaves.bit_length() - 1)
    blocks = LOCAL + crossing
    devices = lax.axis_size("row") * lax.axis_size("col")
    place = jnp.reshape(lax.axis_index(BOTH), (1,))
    upward = [(index, index + 1) for index in range(devices - 1)]
    downward = [(index + 1, index) for index in range(devices - 1)]

    def halo(head, tail):
        return lax.ppermute(tail, BOTH, upward), lax.ppermute(head, BOTH, downward)

    before, after = halo(coords[:, :LEAF], coords[:, width - LEAF :])
    wide = jnp.concatenate([before, coords, after], axis=1)
    near_high, near_low = call(kernel_matrices, [bf16(2 * leaves + 1, LEAF, LEAF)] * 2, wide, wide.T)
    high, low = split_basis(basis)
    nugget = nugget[None, :]
    scalars = [whole(pltpu.SMEM), whole(pltpu.SMEM)]

    solution, field, edges, carried = None, rhs, (rhs[:, :LEAF], rhs[:, width - LEAF :]), None
    for step in range(ITERS):
        first, last = step == 0, step == ITERS - 1
        before, after = halo(*edges)
        (skel,) = call(down_kernel, [f32(rows, blocks * LANES)], field, high, low)
        extra = [] if first else [carried[0], carried[1], carried[2]]
        args = [place, near_ids, field, before, after, nugget, near_high, near_low, skel] + extra
        near, message = call(
            functools.partial(near_kernel, first),
            [f32(rows, width), f32(rows, (crossing + 1) * LANES)],
            *args,
            specs=scalars + [whole()] * (len(args) - 2),
        )
        summed = []
        for bit in range(crossing):
            pairs = [(source, source ^ 2**bit) for source in range(devices)]
            args = [message, lax.ppermute(message, BOTH, pairs)]
            if not first:
                block = (LOCAL + bit) * LANES
                args.append(carried[2][:, block : block + LANES])
            message, level = call(
                functools.partial(combine_kernel, first, LEAF * leaves * 2 ** (bit + 1)),
                [f32(rows, (crossing - bit) * LANES), f32(rows, LANES)],
                *args,
            )
            summed.append(level)
        args = [high, low, near, field, message, skel] + summed
        if not first:
            args = args + [solution, *carried]
        outs = [f32(rows, width)] * 2
        if not last:
            outs = outs + [f32(rows, width)] * 2 + [f32(rows, blocks * LANES), f32(rows, LANES)] + [f32(rows, LEAF)] * 2
        out = call(functools.partial(up_kernel, first, last, crossing), outs, *args)
        solution, field = out[:2]
        if not last:
            carried = out[2:6]
            edges = out[6:8]
    return (solution, field)


def solution(mesh):
    placed = (
        P(None, BOTH),
        P(None, BOTH),
        P(BOTH),
        P(BOTH, None),
        P(None, None, BOTH),
    )
    return jax.shard_map(
        per_device,
        mesh=mesh,
        in_specs=placed,
        out_specs=(P(None, BOTH), P(None, BOTH)),
        check_vma=False,
    )
```

time: 693 us -> 174 us (0.25)
  blocking collectives: 362 us -> 0 us
  matrix products: 184 us -> 0 us
  waiting for transfers between devices: 3.06 us -> 48.7 us
  Pallas kernels: 0 us -> 44.6 us
  other arithmetic: 40.5 us -> 0 us
  starting transfers between devices: 79.1 us -> 66.3 us
    psum x9 -> x0, blocking collectives: 362 us -> none  [the longest x5 205 us: squares(): return lax.psum(jnp.sum(values * values, axis=1), ('row', 'col'))]
    dot_general x68 -> x0, matrix products: 184 us -> none  [the longest x12 75 us: near_field(): jnp.einsum('bij,rbj->rbi', tile_list[offset], segment, precision=lax.Prec...]
    ppermute x70 -> x30, waiting for transfers between devices: 3.06 us -> 48.7 us  [the longest x20 44.3 us: per_device(): args = [message, lax.ppermute(message, BOTH, pairs)]]
    pallas_call x0 -> x34, Pallas kernels: none -> 44.6 us  [the longest x33 43.5 us: call(): pl.pallas_call(body, out_shape=outs, in_specs=specs or [whole()] * len(ar...]
    reduce_sum x9 -> x0, other arithmetic: 39.5 us -> none  [the longest x4 38.3 us: tile_block(): square_dist = jnp.sum(spread * spread, axis=0)]
    ppermute x70 -> x30, starting transfers between devices: 79.1 us -> 66.3 us  [the longest x20 47.6 us: per_device(): args = [message, lax.ppermute(message, BOTH, pairs)]]
  transfers between devices with their start and end apart: 70 -> 30, of which waited for: 4 -> 23; matrix products, arithmetic and copies ran while one was open for 32% -> 1% of each run, Pallas kernels for 0% -> 13%
where the time goes in v1:
time: 174 us
  starting transfers between devices  66.3 us (38%)
  waiting for transfers between devices  48.7 us (28%)
  Pallas kernels  44.6 us (26%)
  local copies, waits for them, and re-layouts  13 us (7%)
    ppermute x20, starting transfers between devices, per_device(): args = [message, lax.ppermute(message, BOTH, pairs)]  47.6 us
    ppermute x20, waiting for transfers between devices, per_device(): args = [message, lax.ppermute(message, BOTH, pairs)]  44.3 us
    pallas_call x33, Pallas kernels, call(): pl.pallas_call(body, out_shape=outs, in_specs=specs or [whole()] * len(ar...  43.5 us
    ppermute x5, starting transfers between devices, halo(): lax.ppermute(tail, BOTH, upward)  12 us
    unnamed x24, local copies, waits for them, and re-layouts  10.8 us
    ppermute x5, starting transfers between devices, halo(): lax.ppermute(head, BOTH, downward)  6.63 us
    ppermute x5, waiting for transfers between devices, halo(): lax.ppermute(head, BOTH, downward)  4.32 us
  transfers between devices with their start and end apart: 30, of which 23 were waited for; matrix products, arithmetic and copies ran while one was open for 1% of the time, Pallas kernels for 13%

profile of v1, /device:TPU:0, one launch (start us, length us, event | category | flops | bytes accessed | tf_op | source)
XLA Modules:
  0.0 173.5 jit_solution(14207355685776386860)
XLA Ops:
  2.7 3.0 %collective-permute-start.2 = (f32[3,512]{1,0:T(4,128)S(1)}, f32[3,512]{1,0:T(4,128)S(1)}, u32[]{:S(2)}, u32[]{:S(2)}) collective-permute-start(f32[3,512]{1,0:T(4,128)S(1)} %get-tuple-element.172), channel_id=1, source_target_pairs={{0,1},{1,2},{2,3},{3,4},{4,5},{5,6},{6,7},{7,8},{8,9},{9,10},{10,1... | collective-permute-start | bytes 18440 | tf_op jit(solution)/shard_map/ppermute | solution.py:263
  7.9 5.1 %collective-permute-start = (f32[32,512]{1,0:T(8,128)S(1)}, f32[32,512]{1,0:T(8,128)S(1)}, u32[]{:S(2)}, u32[]{:S(2)}) collective-permute-start(f32[32,512]{1,0:T(8,128)S(1)} %get-tuple-element.155), channel_id=1, source_target_pairs={{0,1},{1,2},{2,3},{3,4},{4,5},{5,6},{6,7},{7,8},{8,9},{9,10},{10,1... | collective-permute-start | bytes 196616 | tf_op jit(solution)/shard_map/ppermute | solution.py:263
  13.0 3.1 %copy-done.6 = f32[7,128,2048]{2,1,0:T(8,128)S(1)} copy-done((f32[7,128,2048]{2,1,0:T(8,128)S(1)}, f32[7,128,2048]{2,1,0:T(8,128)}, u32[]{:S(2)}) %copy-start.6) | copy-done | bytes 7340056
  27.8 12.3 %shard_map.69 = (bf16[9,512,512]{2,1,0:T(8,128)(2,1)S(1)}, bf16[9,512,512]{2,1,0:T(8,128)(2,1)S(1)}) custom-call(f32[3,3072]{1,0:T(4,128)S(1)} %constant_dynamic-update-slice_fusion.lane_ref, f32[3072,3]{1,0:T(8,128)S(1)} %bitcast.3), custom_call_target="tpu_custom_call" | custom-call | bytes 1048576 | tf_op jit(solution)/shard_map/pallas_call | solution.py:61
  40.2 3.4 %shard_map.71 = (f32[32,2048]{1,0:T(8,128)S(1)}, f32[32,768]{1,0:T(8,128)S(1)}) custom-call(s32[1]{0:T(128)} %bitcast.refs_0_, s32[4,3]{1,0:T(4,128)S(1)} %copy-done.9, f32[32,2048]{1,0:T(8,128)S(1)} %copy-done.7, f32[32,512]{1,0:T(8,128)S(1)} %collective-permute-done.refs_3_, f32[32,512]{1,0:T(8,128)S(1)} %collective-permute-done.1.refs_4_, ...), custom_call_target="tpu_custom_call" | custom-call | bytes 1048576 | tf_op jit(solution)/shard_map/pallas_call | solution.py:61
  46.5 3.3 %collective-permute-start.5 = (f32[32,640]{1,0:T(8,128)S(1)}, f32[32,640]{1,0:T(8,128)S(1)}, u32[]{:S(2)}, u32[]{:S(2)}) collective-permute-start(f32[32,640]{1,0:T(8,128)S(1)} %get-tuple-element.84.refs_0_), channel_id=1, source_target_pairs={{0,2},{1,3},{2,0},{3,1},{4,6},{5,7},{6,4},{7,5},{8,10},{9,11},{10,... | collective-permute-start | bytes 245768 | tf_op jit(solution)/shard_map/ppermute | solution.py:288
  49.7 3.0 %collective-permute-done.5.refs_1_ = f32[32,640]{1,0:T(8,128)S(1)} collective-permute-done((f32[32,640]{1,0:T(8,128)S(1)}, f32[32,640]{1,0:T(8,128)S(1)}, u32[]{:S(2)}, u32[]{:S(2)}) %collective-permute-start.5) | collective-permute-done | bytes 81952 | tf_op jit(solution)/shard_map/ppermute | solution.py:288
  52.8 3.3 %collective-permute-start.6 = (f32[32,512]{1,0:T(8,128)S(1)}, f32[32,512]{1,0:T(8,128)S(1)}, u32[]{:S(2)}, u32[]{:S(2)}) collective-permute-start(f32[32,512]{1,0:T(8,128)S(1)} %get-tuple-element.85.refs_0_), channel_id=1, source_target_pairs={{0,4},{1,5},{2,6},{3,7},{4,0},{5,1},{6,2},{7,3},{8,12},{9,13},{10,... | collective-permute-start | bytes 196616 | tf_op jit(solution)/shard_map/ppermute | solution.py:288
  60.0 2.5 %collective-permute-done.7.refs_1_ = f32[32,384]{1,0:T(8,128)S(1)} collective-permute-done((f32[32,384]{1,0:T(8,128)S(1)}, f32[32,384]{1,0:T(8,128)S(1)}, u32[]{:S(2)}, u32[]{:S(2)}) %collective-permute-start.7) | collective-permute-done | bytes 49184 | tf_op jit(solution)/shard_map/ppermute | solution.py:288
  62.6 2.6 %collective-permute-start.8 = (f32[32,256]{1,0:T(8,128)S(1)}, f32[32,256]{1,0:T(8,128)S(1)}, u32[]{:S(2)}, u32[]{:S(2)}) collective-permute-start(f32[32,256]{1,0:T(8,128)S(1)} %get-tuple-element.87.refs_0_), channel_id=1, source_target_pairs={{0,16},{1,17},{2,18},{3,19},{4,20},{5,21},{6,22},{7,23},{8,24},{9,... | collective-permute-start | bytes 98312 | tf_op jit(solution)/shard_map/ppermute | solution.py:288
  75.4 3.5 %shard_map.79 = (f32[32,2048]{1,0:T(8,128)S(1)}, f32[32,768]{1,0:T(8,128)S(1)}) custom-call(s32[1]{0:T(128)} %bitcast.refs_0_, s32[4,3]{1,0:T(4,128)S(1)} %copy-done.9, f32[32,2048]{1,0:T(8,128)S(1)} %get-tuple-element.94.field_ref.refs_2_.refs_3_, f32[32,512]{1,0:T(8,128)S(1)} %collective-permute-done.9.refs_3_, ...), custom_call_target="tpu_custom_call" | custom-call | bytes 1048576 | tf_op jit(solution)/shard_map/pallas_call | solution.py:61
  78.8 3.0 %collective-permute-start.11 = (f32[32,768]{1,0:T(8,128)S(1)}, f32[32,768]{1,0:T(8,128)S(1)}, u32[]{:S(2)}, u32[]{:S(2)}) collective-permute-start(f32[32,768]{1,0:T(8,128)S(1)} %get-tuple-element.101.refs_0_), channel_id=1, source_target_pairs={{0,1},{1,0},{2,3},{3,2},{4,5},{5,4},{6,7},{7,6},{8,9},{9,8},{10,11... | collective-permute-start | bytes 294920 | tf_op jit(solution)/shard_map/ppermute | solution.py:288
  82.8 2.7 %collective-permute-start.12 = (f32[32,640]{1,0:T(8,128)S(1)}, f32[32,640]{1,0:T(8,128)S(1)}, u32[]{:S(2)}, u32[]{:S(2)}) collective-permute-start(f32[32,640]{1,0:T(8,128)S(1)} %get-tuple-element.102.refs_0_), channel_id=1, source_target_pairs={{0,2},{1,3},{2,0},{3,1},{4,6},{5,7},{6,4},{7,5},{8,10},{9,11},{10,... | collective-permute-start | bytes 245768 | tf_op jit(solution)/shard_map/ppermute | solution.py:288
  85.6 3.0 %collective-permute-done.12.refs_1_ = f32[32,640]{1,0:T(8,128)S(1)} collective-permute-done((f32[32,640]{1,0:T(8,128)S(1)}, f32[32,640]{1,0:T(8,128)S(1)}, u32[]{:S(2)}, u32[]{:S(2)}) %collective-permute-start.12) | collective-permute-done | bytes 81952 | tf_op jit(solution)/shard_map/ppermute | solution.py:288
  97.2 2.6 %collective-permute-start.15 = (f32[32,256]{1,0:T(8,128)S(1)}, f32[32,256]{1,0:T(8,128)S(1)}, u32[]{:S(2)}, u32[]{:S(2)}) collective-permute-start(f32[32,256]{1,0:T(8,128)S(1)} %get-tuple-element.105.refs_0_), channel_id=1, source_target_pairs={{0,16},{1,17},{2,18},{3,19},{4,20},{5,21},{6,22},{7,23},{8,24},{9,... | collective-permute-start | bytes 98312 | tf_op jit(solution)/shard_map/ppermute | solution.py:288
  110.0 3.5 %shard_map.87 = (f32[32,2048]{1,0:T(8,128)S(1)}, f32[32,768]{1,0:T(8,128)S(1)}) custom-call(s32[1]{0:T(128)} %bitcast.refs_0_, s32[4,3]{1,0:T(4,128)S(1)} %copy-done.9, f32[32,2048]{1,0:T(8,128)S(1)} %get-tuple-element.114.field_ref.refs_2_.refs_3_, f32[32,512]{1,0:T(8,128)S(1)} %collective-permute-done.16.refs_3_, ...), custom_call_target="tpu_custom_call" | custom-call | bytes 1048576 | tf_op jit(solution)/shard_map/pallas_call | solution.py:61
  113.5 3.0 %collective-permute-start.18 = (f32[32,768]{1,0:T(8,128)S(1)}, f32[32,768]{1,0:T(8,128)S(1)}, u32[]{:S(2)}, u32[]{:S(2)}) collective-permute-start(f32[32,768]{1,0:T(8,128)S(1)} %get-tuple-element.121.refs_0_), channel_id=1, source_target_pairs={{0,1},{1,0},{2,3},{3,2},{4,5},{5,4},{6,7},{7,6},{8,9},{9,8},{10,11... | collective-permute-start | bytes 294920 | tf_op jit(solution)/shard_map/ppermute | solution.py:288
  117.5 2.6 %collective-permute-start.19 = (f32[32,640]{1,0:T(8,128)S(1)}, f32[32,640]{1,0:T(8,128)S(1)}, u32[]{:S(2)}, u32[]{:S(2)}) collective-permute-start(f32[32,640]{1,0:T(8,128)S(1)} %get-tuple-element.122.refs_0_), channel_id=1, source_target_pairs={{0,2},{1,3},{2,0},{3,1},{4,6},{5,7},{6,4},{7,5},{8,10},{9,11},{10,... | collective-permute-start | bytes 245768 | tf_op jit(solution)/shard_map/ppermute | solution.py:288
  120.1 3.0 %collective-permute-done.19.refs_1_ = f32[32,640]{1,0:T(8,128)S(1)} collective-permute-done((f32[32,640]{1,0:T(8,128)S(1)}, f32[32,640]{1,0:T(8,128)S(1)}, u32[]{:S(2)}, u32[]{:S(2)}) %collective-permute-start.19) | collective-permute-done | bytes 81952 | tf_op jit(solution)/shard_map/ppermute | solution.py:288
  144.6 3.4 %shard_map.95 = (f32[32,2048]{1,0:T(8,128)S(1)}, f32[32,768]{1,0:T(8,128)S(1)}) custom-call(s32[1]{0:T(128)} %bitcast.refs_0_, s32[4,3]{1,0:T(4,128)S(1)} %copy-done.9, f32[32,2048]{1,0:T(8,128)S(1)} %get-tuple-element.134.field_ref.refs_2_.refs_3_, f32[32,512]{1,0:T(8,128)S(1)} %collective-permute-done.23.refs_3_, ...), custom_call_target="tpu_custom_call" | custom-call | bytes 1048576 | tf_op jit(solution)/shard_map/pallas_call | solution.py:61
  148.1 3.0 %collective-permute-start.25 = (f32[32,768]{1,0:T(8,128)S(1)}, f32[32,768]{1,0:T(8,128)S(1)}, u32[]{:S(2)}, u32[]{:S(2)}) collective-permute-start(f32[32,768]{1,0:T(8,128)S(1)} %get-tuple-element.141.refs_0_), channel_id=1, source_target_pairs={{0,1},{1,0},{2,3},{3,2},{4,5},{5,4},{6,7},{7,6},{8,9},{9,8},{10,11... | collective-permute-start | bytes 294920 | tf_op jit(solution)/shard_map/ppermute | solution.py:288
  152.1 2.7 %collective-permute-start.26 = (f32[32,640]{1,0:T(8,128)S(1)}, f32[32,640]{1,0:T(8,128)S(1)}, u32[]{:S(2)}, u32[]{:S(2)}) collective-permute-start(f32[32,640]{1,0:T(8,128)S(1)} %get-tuple-element.142.refs_0_), channel_id=1, source_target_pairs={{0,2},{1,3},{2,0},{3,1},{4,6},{5,7},{6,4},{7,5},{8,10},{9,11},{10,... | collective-permute-start | bytes 245768 | tf_op jit(solution)/shard_map/ppermute | solution.py:288
  154.8 3.0 %collective-permute-done.26.refs_1_ = f32[32,640]{1,0:T(8,128)S(1)} collective-permute-done((f32[32,640]{1,0:T(8,128)S(1)}, f32[32,640]{1,0:T(8,128)S(1)}, u32[]{:S(2)}, u32[]{:S(2)}) %collective-permute-start.26) | collective-permute-done | bytes 81952 | tf_op jit(solution)/shard_map/ppermute | solution.py:288
  168.6 2.7 %collective-permute-done.29.refs_1_ = f32[32,256]{1,0:T(8,128)S(1)} collective-permute-done((f32[32,256]{1,0:T(8,128)S(1)}, f32[32,256]{1,0:T(8,128)S(1)}, u32[]{:S(2)}, u32[]{:S(2)}) %collective-permute-start.29) | collective-permute-done | bytes 32800 | tf_op jit(solution)/shard_map/ppermute | solution.py:288
  (101 shorter events, 89.3 us)
Async XLA Ops:
  1.4 25.9 %collective-permute-start.3 = (f32[3,512]{1,0:T(4,128)S(1)}, f32[3,512]{1,0:T(4,128)S(1)}, u32[]{:S(2)}, u32[]{:S(2)}) collective-permute-start(f32[3,512]{1,0:T(4,128)S(1)} %get-tuple-element.171), channel_id=1, source_target_pairs={{1,0},{2,1},{3,2},{4,3},{5,4},{6,5},{7,6},{8,7},{9,8},{10,9},{11,1... | collective-permute-start | bytes 18440 | tf_op jit(solution)/shard_map/ppermute | solution.py:263
  2.7 24.5 %collective-permute-start.2 = (f32[3,512]{1,0:T(4,128)S(1)}, f32[3,512]{1,0:T(4,128)S(1)}, u32[]{:S(2)}, u32[]{:S(2)}) collective-permute-start(f32[3,512]{1,0:T(4,128)S(1)} %get-tuple-element.172), channel_id=1, source_target_pairs={{0,1},{1,2},{2,3},{3,4},{4,5},{5,6},{6,7},{7,8},{8,9},{9,10},{10,1... | collective-permute-start | bytes 18440 | tf_op jit(solution)/shard_map/ppermute | solution.py:263
  6.6 33.5 %collective-permute-start.1 = (f32[32,512]{1,0:T(8,128)S(1)}, f32[32,512]{1,0:T(8,128)S(1)}, u32[]{:S(2)}, u32[]{:S(2)}) collective-permute-start(f32[32,512]{1,0:T(8,128)S(1)} %get-tuple-element.154), channel_id=1, source_target_pairs={{1,0},{2,1},{3,2},{4,3},{5,4},{6,5},{7,6},{8,7},{9,8},{10,9},{11,1... | collective-permute-start | bytes 196616 | tf_op jit(solution)/shard_map/ppermute | solution.py:263
  7.9 32.2 %collective-permute-start = (f32[32,512]{1,0:T(8,128)S(1)}, f32[32,512]{1,0:T(8,128)S(1)}, u32[]{:S(2)}, u32[]{:S(2)}) collective-permute-start(f32[32,512]{1,0:T(8,128)S(1)} %get-tuple-element.155), channel_id=1, source_target_pairs={{0,1},{1,2},{2,3},{3,4},{4,5},{5,6},{6,7},{7,8},{8,9},{9,10},{10,1... | collective-permute-start | bytes 196616 | tf_op jit(solution)/shard_map/ppermute | solution.py:263
  46.5 6.2 %collective-permute-start.5 = (f32[32,640]{1,0:T(8,128)S(1)}, f32[32,640]{1,0:T(8,128)S(1)}, u32[]{:S(2)}, u32[]{:S(2)}) collective-permute-start(f32[32,640]{1,0:T(8,128)S(1)} %get-tuple-element.84.refs_0_), channel_id=1, source_target_pairs={{0,2},{1,3},{2,0},{3,1},{4,6},{5,7},{6,4},{7,5},{8,10},{9,11},{10,... | collective-permute-start | bytes 245768 | tf_op jit(solution)/shard_map/ppermute | solution.py:288
  52.8 5.6 %collective-permute-start.6 = (f32[32,512]{1,0:T(8,128)S(1)}, f32[32,512]{1,0:T(8,128)S(1)}, u32[]{:S(2)}, u32[]{:S(2)}) collective-permute-start(f32[32,512]{1,0:T(8,128)S(1)} %get-tuple-element.85.refs_0_), channel_id=1, source_target_pairs={{0,4},{1,5},{2,6},{3,7},{4,0},{5,1},{6,2},{7,3},{8,12},{9,13},{10,... | collective-permute-start | bytes 196616 | tf_op jit(solution)/shard_map/ppermute | solution.py:288
  62.6 4.8 %collective-permute-start.8 = (f32[32,256]{1,0:T(8,128)S(1)}, f32[32,256]{1,0:T(8,128)S(1)}, u32[]{:S(2)}, u32[]{:S(2)}) collective-permute-start(f32[32,256]{1,0:T(8,128)S(1)} %get-tuple-element.87.refs_0_), channel_id=1, source_target_pairs={{0,16},{1,17},{2,18},{3,19},{4,20},{5,21},{6,22},{7,23},{8,24},{9,... | collective-permute-start | bytes 98312 | tf_op jit(solution)/shard_map/ppermute | solution.py:288
  68.9 4.9 %collective-permute-start.9 = (f32[32,512]{1,0:T(8,128)S(1)}, f32[32,512]{1,0:T(8,128)S(1)}, u32[]{:S(2)}, u32[]{:S(2)}) collective-permute-start(f32[32,512]{1,0:T(8,128)S(1)} %get-tuple-element.95), channel_id=1, source_target_pairs={{0,1},{1,2},{2,3},{3,4},{4,5},{5,6},{6,7},{7,8},{8,9},{9,10},{10,1... | collective-permute-start | bytes 196616 | tf_op jit(solution)/shard_map/ppermute | solution.py:263
  70.2 5.1 %collective-permute-start.10 = (f32[32,512]{1,0:T(8,128)S(1)}, f32[32,512]{1,0:T(8,128)S(1)}, u32[]{:S(2)}, u32[]{:S(2)}) collective-permute-start(f32[32,512]{1,0:T(8,128)S(1)} %get-tuple-element.96), channel_id=1, source_target_pairs={{1,0},{2,1},{3,2},{4,3},{5,4},{6,5},{7,6},{8,7},{9,8},{10,9},{11,1... | collective-permute-start | bytes 196616 | tf_op jit(solution)/shard_map/ppermute | solution.py:263
  82.8 5.7 %collective-permute-start.12 = (f32[32,640]{1,0:T(8,128)S(1)}, f32[32,640]{1,0:T(8,128)S(1)}, u32[]{:S(2)}, u32[]{:S(2)}) collective-permute-start(f32[32,640]{1,0:T(8,128)S(1)} %get-tuple-element.102.refs_0_), channel_id=1, source_target_pairs={{0,2},{1,3},{2,0},{3,1},{4,6},{5,7},{6,4},{7,5},{8,10},{9,11},{10,... | collective-permute-start | bytes 245768 | tf_op jit(solution)/shard_map/ppermute | solution.py:288
  88.6 4.3 %collective-permute-start.13 = (f32[32,512]{1,0:T(8,128)S(1)}, f32[32,512]{1,0:T(8,128)S(1)}, u32[]{:S(2)}, u32[]{:S(2)}) collective-permute-start(f32[32,512]{1,0:T(8,128)S(1)} %get-tuple-element.103.refs_0_), channel_id=1, source_target_pairs={{0,4},{1,5},{2,6},{3,7},{4,0},{5,1},{6,2},{7,3},{8,12},{9,13},{10,... | collective-permute-start | bytes 196616 | tf_op jit(solution)/shard_map/ppermute | solution.py:288
  93.0 4.2 %collective-permute-start.14 = (f32[32,384]{1,0:T(8,128)S(1)}, f32[32,384]{1,0:T(8,128)S(1)}, u32[]{:S(2)}, u32[]{:S(2)}) collective-permute-start(f32[32,384]{1,0:T(8,128)S(1)} %get-tuple-element.104.refs_0_), channel_id=1, source_target_pairs={{0,8},{1,9},{2,10},{3,11},{4,12},{5,13},{6,14},{7,15},{8,0},{9,1},... | collective-permute-start | bytes 147464 | tf_op jit(solution)/shard_map/ppermute | solution.py:288
  97.2 4.8 %collective-permute-start.15 = (f32[32,256]{1,0:T(8,128)S(1)}, f32[32,256]{1,0:T(8,128)S(1)}, u32[]{:S(2)}, u32[]{:S(2)}) collective-permute-start(f32[32,256]{1,0:T(8,128)S(1)} %get-tuple-element.105.refs_0_), channel_id=1, source_target_pairs={{0,16},{1,17},{2,18},{3,19},{4,20},{5,21},{6,22},{7,23},{8,24},{9,... | collective-permute-start | bytes 98312 | tf_op jit(solution)/shard_map/ppermute | solution.py:288
  103.6 5.1 %collective-permute-start.16 = (f32[32,512]{1,0:T(8,128)S(1)}, f32[32,512]{1,0:T(8,128)S(1)}, u32[]{:S(2)}, u32[]{:S(2)}) collective-permute-start(f32[32,512]{1,0:T(8,128)S(1)} %get-tuple-element.115), channel_id=1, source_target_pairs={{0,1},{1,2},{2,3},{3,4},{4,5},{5,6},{6,7},{7,8},{8,9},{9,10},{10,1... | collective-permute-start | bytes 196616 | tf_op jit(solution)/shard_map/ppermute | solution.py:263
  104.9 5.1 %collective-permute-start.17 = (f32[32,512]{1,0:T(8,128)S(1)}, f32[32,512]{1,0:T(8,128)S(1)}, u32[]{:S(2)}, u32[]{:S(2)}) collective-permute-start(f32[32,512]{1,0:T(8,128)S(1)} %get-tuple-element.116), channel_id=1, source_target_pairs={{1,0},{2,1},{3,2},{4,3},{5,4},{6,5},{7,6},{8,7},{9,8},{10,9},{11,1... | collective-permute-start | bytes 196616 | tf_op jit(solution)/shard_map/ppermute | solution.py:263
  117.5 5.6 %collective-permute-start.19 = (f32[32,640]{1,0:T(8,128)S(1)}, f32[32,640]{1,0:T(8,128)S(1)}, u32[]{:S(2)}, u32[]{:S(2)}) collective-permute-start(f32[32,640]{1,0:T(8,128)S(1)} %get-tuple-element.122.refs_0_), channel_id=1, source_target_pairs={{0,2},{1,3},{2,0},{3,1},{4,6},{5,7},{6,4},{7,5},{8,10},{9,11},{10,... | collective-permute-start | bytes 245768 | tf_op jit(solution)/shard_map/ppermute | solution.py:288
  123.2 4.3 %collective-permute-start.20 = (f32[32,512]{1,0:T(8,128)S(1)}, f32[32,512]{1,0:T(8,128)S(1)}, u32[]{:S(2)}, u32[]{:S(2)}) collective-permute-start(f32[32,512]{1,0:T(8,128)S(1)} %get-tuple-element.123.refs_0_), channel_id=1, source_target_pairs={{0,4},{1,5},{2,6},{3,7},{4,0},{5,1},{6,2},{7,3},{8,12},{9,13},{10,... | collective-permute-start | bytes 196616 | tf_op jit(solution)/shard_map/ppermute | solution.py:288
  127.6 4.2 %collective-permute-start.21 = (f32[32,384]{1,0:T(8,128)S(1)}, f32[32,384]{1,0:T(8,128)S(1)}, u32[]{:S(2)}, u32[]{:S(2)}) collective-permute-start(f32[32,384]{1,0:T(8,128)S(1)} %get-tuple-element.124.refs_0_), channel_id=1, source_target_pairs={{0,8},{1,9},{2,10},{3,11},{4,12},{5,13},{6,14},{7,15},{8,0},{9,1},... | collective-permute-start | bytes 147464 | tf_op jit(solution)/shard_map/ppermute | solution.py:288
  131.8 4.8 %collective-permute-start.22 = (f32[32,256]{1,0:T(8,128)S(1)}, f32[32,256]{1,0:T(8,128)S(1)}, u32[]{:S(2)}, u32[]{:S(2)}) collective-permute-start(f32[32,256]{1,0:T(8,128)S(1)} %get-tuple-element.125.refs_0_), channel_id=1, source_target_pairs={{0,16},{1,17},{2,18},{3,19},{4,20},{5,21},{6,22},{7,23},{8,24},{9,... | collective-permute-start | bytes 98312 | tf_op jit(solution)/shard_map/ppermute | solution.py:288
  138.2 4.9 %collective-permute-start.23 = (f32[32,512]{1,0:T(8,128)S(1)}, f32[32,512]{1,0:T(8,128)S(1)}, u32[]{:S(2)}, u32[]{:S(2)}) collective-permute-start(f32[32,512]{1,0:T(8,128)S(1)} %get-tuple-element.135), channel_id=1, source_target_pairs={{0,1},{1,2},{2,3},{3,4},{4,5},{5,6},{6,7},{7,8},{8,9},{9,10},{10,1... | collective-permute-start | bytes 196616 | tf_op jit(solution)/shard_map/ppermute | solution.py:263
  139.5 5.1 %collective-permute-start.24 = (f32[32,512]{1,0:T(8,128)S(1)}, f32[32,512]{1,0:T(8,128)S(1)}, u32[]{:S(2)}, u32[]{:S(2)}) collective-permute-start(f32[32,512]{1,0:T(8,128)S(1)} %get-tuple-element.136), channel_id=1, source_target_pairs={{1,0},{2,1},{3,2},{4,3},{5,4},{6,5},{7,6},{8,7},{9,8},{10,9},{11,1... | collective-permute-start | bytes 196616 | tf_op jit(solution)/shard_map/ppermute | solution.py:263
  152.1 5.7 %collective-permute-start.26 = (f32[32,640]{1,0:T(8,128)S(1)}, f32[32,640]{1,0:T(8,128)S(1)}, u32[]{:S(2)}, u32[]{:S(2)}) collective-permute-start(f32[32,640]{1,0:T(8,128)S(1)} %get-tuple-element.142.refs_0_), channel_id=1, source_target_pairs={{0,2},{1,3},{2,0},{3,1},{4,6},{5,7},{6,4},{7,5},{8,10},{9,11},{10,... | collective-permute-start | bytes 245768 | tf_op jit(solution)/shard_map/ppermute | solution.py:288
  157.9 4.3 %collective-permute-start.27 = (f32[32,512]{1,0:T(8,128)S(1)}, f32[32,512]{1,0:T(8,128)S(1)}, u32[]{:S(2)}, u32[]{:S(2)}) collective-permute-start(f32[32,512]{1,0:T(8,128)S(1)} %get-tuple-element.143.refs_0_), channel_id=1, source_target_pairs={{0,4},{1,5},{2,6},{3,7},{4,0},{5,1},{6,2},{7,3},{8,12},{9,13},{10,... | collective-permute-start | bytes 196616 | tf_op jit(solution)/shard_map/ppermute | solution.py:288
  166.5 4.8 %collective-permute-start.29 = (f32[32,256]{1,0:T(8,128)S(1)}, f32[32,256]{1,0:T(8,128)S(1)}, u32[]{:S(2)}, u32[]{:S(2)}) collective-permute-start(f32[32,256]{1,0:T(8,128)S(1)} %get-tuple-element.145.refs_0_), channel_id=1, source_target_pairs={{0,16},{1,17},{2,18},{3,19},{4,20},{5,21},{6,22},{7,23},{8,24},{9,... | collective-permute-start | bytes 98312 | tf_op jit(solution)/shard_map/ppermute | solution.py:288
  (17 other events, 150.1 us)

commit v2 on v1

--- a/solution.py
+++ b/solution.py
@@ -119,24 +119,28 @@
     lax.fori_loop(0, (2 * leaves + 1) * parts, one, 0)
 
 
-def down_kernel(field_ref, high_ref, low_ref, out_ref):
+def down_kernel(field_ref, high_ref, low_ref, local_ref, out_ref):
     rank = LANES
     half = field_ref.shape[1] // 2
     stack = stacked(field_ref[...])
     for part in range(2):
         points = slice(part * half, (part + 1) * half)
-        out_ref[:, part * rank : (part + 1) * rank] = product(
+        local_ref[:, part * rank : (part + 1) * rank] = product(
             stack[:, points], high_ref[:rank, points], low_ref[:rank, points], ROWS_ROWS
         )
-    out_ref[:, 2 * rank :] = product(stack, high_ref[rank:], low_ref[rank:], ROWS_ROWS)
+    whole_width = product(stack, high_ref[rank:], low_ref[rank:], ROWS_ROWS)
+    local_ref[:, 2 * rank :] = whole_width[:, :rank]
+    out_ref[...] = jnp.zeros(out_ref.shape, jnp.float32)
+    for bit in range(whole_width.shape[1] // rank - 1):
+        out_ref[:, bit, :] = whole_width[:, (bit + 1) * rank : (bit + 2) * rank]
 
 
 def near_kernel(first, *refs):
     (place_ref, ids_ref, field_ref, before_ref, after_ref, nugget_ref, high_ref, low_ref, skel_ref) = refs[:9]
     if first:
-        out_ref, message_ref = refs[9:]
+        out_ref, sums_ref = refs[9:]
     else:
-        direction_ref, image_ref, old_skel_ref, out_ref, message_ref = refs[9:]
+        direction_ref, image_ref, old_skel_ref, out_ref, sums_ref = refs[9:]
     rows, width = field_ref.shape
     leaves = width // LEAF
 
@@ -152,7 +156,7 @@
 
     pieces = [stacked(before_ref[...])] + [stacked(own(field_ref, leaf)) for leaf in range(leaves)]
     pieces = pieces + [stacked(after_ref[...])]
-    square = with_image = cross = 0.0
+    square = with_image = cross = jnp.zeros((rows, 1), jnp.float32)
     for leaf in range(leaves):
         field = own(field_ref, leaf)
         before = product(pieces[leaf], high_ref[leaves + leaf], low_ref[leaves + leaf], ROWS_COLS)
@@ -171,33 +175,58 @@
         with_image = with_image + scale * row_sum(skel_ref[:, here] * skel_ref[:, here])
         if not first:
             cross = cross + scale * row_sum(skel_ref[:, here] * old_skel_ref[:, here])
-    wide = message_ref.shape[1] - LANES
-    message_ref[:, :wide] = skel_ref[:, LOCAL * LANES :]
-    message_ref[:, wide:] = in_lanes([square, with_image, cross], (rows, LANES))
-
-
-def combine_kernel(first, cluster, *refs):
-    if first:
-        mine_ref, other_ref, next_ref, level_ref = refs
-    else:
-        mine_ref, other_ref, old_ref, next_ref, level_ref = refs
-    total = mine_ref[...] + other_ref[...]
-    level = total[:, :LANES]
-    level_ref[...] = level
-    columns = [0.0, row_sum(level * level) * (1.0 / cluster)]
-    if not first:
-        columns.append(row_sum(level * old_ref[...]) * (1.0 / cluster))
-    wide = total.shape[1] - 2 * LANES
-    if wide:
-        next_ref[:, :wide] = total[:, LANES : LANES + wide]
-    next_ref[:, wide:] = total[:, LANES + wide :] + in_lanes(columns, level.shape)
+    sums_ref[...] = in_lanes([square, with_image, cross], (rows, LANES))
+
+
+def middle_kernel(step, crossing, parts, cluster, *refs):
+    refs = list(refs)
+    place_ref, gathered_ref, sums_ref = refs[:3]
+    previous_ref = refs[3] if step >= 1 else None
+    older_ref, state_ref = refs[4:6] if step >= 2 else (None, None)
+    outs = refs[3 + (step >= 1) + 2 * (step >= 2) :]
+    out_ref = outs[0]
+    devices, depth, _ = gathered_ref.shape
+    shape = (1, depth, LANES)
+    level = lax.broadcasted_iota(jnp.int32, shape, 1)
+    lane = lax.broadcasted_iota(jnp.int32, shape, 2)
+    mine = place_ref[0] // parts
+    sums = gathered_ref[...]
+    spread = jnp.zeros(sums.shape, jnp.float32)
+    weight = jnp.zeros(shape, jnp.float32)
+    for bit in range(crossing):
+        pair = sums.reshape(devices >> (bit + 1), 2, depth, LANES)
+        sums = pair[:, 0] + pair[:, 1]
+        copies = jnp.broadcast_to(sums[:, None], (devices >> (bit + 1), 2 << bit, depth, LANES))
+        spread = jnp.where(level == bit, copies.reshape(devices, depth, LANES), spread)
+        weight = jnp.where(level == bit, 1.0 / (cluster * (2 << bit) * (2 << bit)), weight)
+
+    def whole_sum(values):
+        return jnp.sum(jnp.sum(values, axis=0), keepdims=True)[None]
+
+    with_image = whole_sum(spread * spread * weight)
+    cross = jnp.zeros((1, 1, 1), jnp.float32)
+    if step >= 1:
+        old = previous_ref[...]
+        if step >= 2:
+            old = old + state_ref[pl.ds(mine, 1), 2:3][None] * older_ref[...]
+        cross = whole_sum(spread * old * weight)
+        if len(outs) == 2:
+            outs[1][...] = old
+    here = jnp.zeros((sums_ref.shape[0], LANES), jnp.float32)
+    lanes = lax.broadcasted_iota(jnp.int32, here.shape, 1)
+    for index in range(3):
+        here = jnp.where(lanes == crossing + index, sums_ref[:, index : index + 1], here)
+    turned = here.T[:depth]
+    turned = jnp.concatenate([turned, jnp.zeros((depth, LANES - turned.shape[1]), jnp.float32)], axis=1)[None]
+    extra = jnp.where(level == crossing + 1, with_image, jnp.where(level == crossing + 2, cross, 0.0))
+    turned = turned + jnp.where(lane == mine, extra, 0.0)
+    out_ref[...] = jnp.where(level < crossing, spread, turned)
 
 
 def up_kernel(first, last, crossing, *refs):
     refs = list(refs)
-    high_ref, low_ref, near_ref, field_ref, sums_ref, skel_ref = refs[:6]
-    level_refs = refs[6 : 6 + crossing]
-    refs = refs[6 + crossing :]
+    high_ref, low_ref, near_ref, field_ref, spread_ref, skel_ref = refs[:6]
+    refs = refs[6:]
     if not first:
         solution_ref, direction_ref, image_ref, old_skel_ref, state_ref = refs[:5]
         refs = refs[5:]
@@ -216,14 +245,16 @@
         ) = refs
     rows, width = field_ref.shape
     half = width // 2
-    norm = sums_ref[:, 0:1]
-    curve = sums_ref[:, 1:2]
+    sums = jnp.sum(spread_ref[...], axis=0).T[:rows]
+    norm = sums[:, crossing : crossing + 1]
+    curve = sums[:, crossing + 1 : crossing + 2]
+    ratio = jnp.zeros_like(norm)
     if not first:
         ratio = norm / state_ref[:, 0:1]
-        curve = curve + ratio * (sums_ref[:, 2:3] + ratio * state_ref[:, 1:2])
+        curve = curve + ratio * (sums[:, crossing + 2 : crossing + 3] + ratio * state_ref[:, 1:2])
     step = norm / curve
     blocks = [skel_ref[:, block * LANES : (block + 1) * LANES] for block in range(LOCAL)]
-    blocks = blocks + [ref[...] for ref in level_refs]
+    blocks = blocks + [spread_ref[:, bit, :] for bit in range(crossing)]
     scaled = [block * (1.0 / (LEAF * (2 ** max(index, 1)))) for index, block in enumerate(blocks)]
     for part in range(2):
         points = slice(part * half, (part + 1) * half)
@@ -242,10 +273,10 @@
     if not last:
         head_ref[...] = new_field_ref[:, :LEAF]
         tail_ref[...] = new_field_ref[:, width - LEAF :]
-        for index, block in enumerate(blocks):
+        for index in range(LOCAL):
             here = slice(index * LANES, (index + 1) * LANES)
-            new_skel_ref[:, here] = block if first else block + ratio * old_skel_ref[:, here]
-        new_state_ref[...] = in_lanes([norm, curve], (rows, LANES))
+            new_skel_ref[:, here] = blocks[index] if first else blocks[index] + ratio * old_skel_ref[:, here]
+        new_state_ref[...] = in_lanes([norm, curve, ratio], (rows, LANES))
 
 
 def per_device(rhs, coords, nugget, near_ids, basis):
@@ -253,54 +284,71 @@
     levels, rank, _ = basis.shape
     leaves = width // LEAF
     crossing = levels - (leaves.bit_length() - 1)
-    blocks = LOCAL + crossing
+    depth = (crossing + 3 + 7) // 8 * 8
     devices = lax.axis_size("row") * lax.axis_size("col")
+    parts = devices // rows
     place = jnp.reshape(lax.axis_index(BOTH), (1,))
     upward = [(index, index + 1) for index in range(devices - 1)]
     downward = [(index + 1, index) for index in range(devices - 1)]
 
     def halo(head, tail):
         return lax.ppermute(tail, BOTH, upward), lax.ppermute(head, BOTH, downward)
+
+    def exchange(blocks):
+        return lax.all_to_all(blocks, BOTH, 0, 0, tiled=True)
+
+    def to_owners(partial):
+        if parts == 1:
+            return exchange(partial)
+        cut = partial.reshape(rows, depth, parts, LANES // parts).transpose(0, 2, 1, 3)
+        got = exchange(cut.reshape(devices, depth, LANES // parts))
+        return jnp.pad(got, ((0, 0), (0, 0), (0, LANES - LANES // parts)))
+
+    def from_owners(spread):
+        got = exchange(spread)
+        if parts == 1:
+            return got
+        got = got.reshape(rows, parts, depth, LANES)
+        skeletons = got[:, :, :crossing, : LANES // parts].transpose(0, 2, 1, 3).reshape(rows, crossing, LANES)
+        return jnp.concatenate([skeletons, jnp.sum(got[:, :, crossing:], axis=1)], axis=1)
 
     before, after = halo(coords[:, :LEAF], coords[:, width - LEAF :])
     wide = jnp.concatenate([before, coords, after], axis=1)
     near_high, near_low = call(kernel_matrices, [bf16(2 * leaves + 1, LEAF, LEAF)] * 2, wide, wide.T)
     high, low = split_basis(basis)
     nugget = nugget[None, :]
-    scalars = [whole(pltpu.SMEM), whole(pltpu.SMEM)]
+    smem = whole(pltpu.SMEM)
 
     solution, field, edges, carried = None, rhs, (rhs[:, :LEAF], rhs[:, width - LEAF :]), None
     for step in range(ITERS):
         first, last = step == 0, step == ITERS - 1
         before, after = halo(*edges)
-        (skel,) = call(down_kernel, [f32(rows, blocks * LANES)], field, high, low)
+        local, partial = call(down_kernel, [f32(rows, LOCAL * LANES), f32(rows, depth, LANES)], field, high, low)
+        gathered = to_owners(partial)
         extra = [] if first else [carried[0], carried[1], carried[2]]
-        args = [place, near_ids, field, before, after, nugget, near_high, near_low, skel] + extra
-        near, message = call(
+        args = [place, near_ids, field, before, after, nugget, near_high, near_low, local] + extra
+        near, sums = call(
             functools.partial(near_kernel, first),
-            [f32(rows, width), f32(rows, (crossing + 1) * LANES)],
+            [f32(rows, width), f32(rows, LANES)],
             *args,
-            specs=scalars + [whole()] * (len(args) - 2),
+            specs=[smem, smem] + [whole()] * (len(args) - 2),
+            flops=2 * 12 * LEAF * LEAF * rows * 8,
         )
-        summed = []
-        for bit in range(crossing):
-            pairs = [(source, source ^ 2**bit) for source in range(devices)]
-            args = [message, lax.ppermute(message, BOTH, pairs)]
-            if not first:
-                block = (LOCAL + bit) * LANES
-                args.append(carried[2][:, block : block + LANES])
-            message, level = call(
-                functools.partial(combine_kernel, first, LEAF * leaves * 2 ** (bit + 1)),
-                [f32(rows, (crossing - bit) * LANES), f32(rows, LANES)],
-                *args,
-            )
-            summed.append(level)
-        args = [high, low, near, field, message, skel] + summed
+        args = [place, gathered, sums] + ([spread] if step >= 1 else []) + ([older, carried[3]] if step >= 2 else [])
+        kept = 1 <= step < ITERS - 1
+        spread, *rest = call(
+            functools.partial(middle_kernel, step, crossing, parts, LEAF * leaves),
+            [f32(devices, depth, LANES)] * (2 if kept else 1),
+            *args,
+            specs=[smem] + [whole()] * (len(args) - 1),
+        )
+        older = rest[0] if kept else None
+        args = [high, low, near, field, from_owners(spread), local]
         if not first:
             args = args + [solution, *carried]
         outs = [f32(rows, width)] * 2
         if not last:
-            outs = outs + [f32(rows, width)] * 2 + [f32(rows, blocks * LANES), f32(rows, LANES)] + [f32(rows, LEAF)] * 2
+            outs = outs + [f32(rows, width)] * 2 + [f32(rows, LOCAL * LANES), f32(rows, LANES)] + [f32(rows, LEAF)] * 2
         out = call(functools.partial(up_kernel, first, last, crossing), outs, *args)
         solution, field = out[:2]
         if not last:

time: 174 us -> 203 us (1.17)
  blocking collectives: 0 us -> 65.1 us
  waiting for transfers between devices: 48.7 us -> 8.79 us
  local copies, waits for them, and re-layouts: 13 us -> 41.7 us
  starting transfers between devices: 66.3 us -> 38.3 us
  Pallas kernels: 44.6 us -> 46.8 us
    all_to_all x0 -> x4, blocking collectives: none -> 65.1 us  [exchange(): return lax.all_to_all(blocks, BOTH, 0, 0, tiled=True)]
    ppermute x20 -> x0, starting transfers between devices: 47.6 us -> none  [per_device(): args = [message, lax.ppermute(message, BOTH, pairs)]]
    ppermute x20 -> x0, waiting for transfers between devices: 44.3 us -> none  [per_device(): args = [message, lax.ppermute(message, BOTH, pairs)]]
    unnamed x24 -> x48, local copies, waits for them, and re-layouts: 10.8 us -> 39.6 us
    all_to_all x0 -> x4, starting transfers between devices: none -> 17.5 us  [exchange(): return lax.all_to_all(blocks, BOTH, 0, 0, tiled=True)]
    ppermute x5, waiting for transfers between devices: 4.32 us -> 8.77 us  [halo(): lax.ppermute(head, BOTH, downward)]
    pallas_call x33 -> x17, Pallas kernels: 43.5 us -> 45.8 us  [call(): pl.pallas_call(body, out_shape=outs, in_specs=specs or [whole()] * len(ar...]
    ppermute x5, starting transfers between devices: 12 us -> 14.2 us  [halo(): lax.ppermute(tail, BOTH, upward)]
  transfers between devices with their start and end apart: 30 -> 14, of which waited for: 23 -> 3; matrix products, arithmetic and copies ran while one was open for 1% -> 1% of each run, Pallas kernels for 13% -> 15%
where the time goes in v2:
time: 203 us; the launch traced here: 202 us
  blocking collectives  65.1 us (32%)
  Pallas kernels  46.8 us (23%)
  local copies, waits for them, and re-layouts  41.7 us (21%)
  starting transfers between devices  38.3 us (19%)
  waiting for transfers between devices  8.79 us (4%)
    all_to_all x4, blocking collectives, exchange(): return lax.all_to_all(blocks, BOTH, 0, 0, tiled=True)  65.1 us
    pallas_call x17, Pallas kernels, call(): pl.pallas_call(body, out_shape=outs, in_specs=specs or [whole()] * len(ar...  45.8 us
    unnamed x48, local copies, waits for them, and re-layouts  39.6 us
    all_to_all x4, starting transfers between devices, exchange(): return lax.all_to_all(blocks, BOTH, 0, 0, tiled=True)  17.5 us
    ppermute x5, starting transfers between devices, halo(): lax.ppermute(tail, BOTH, upward)  14.2 us
    ppermute x5, waiting for transfers between devices, halo(): lax.ppermute(head, BOTH, downward)  8.77 us
    ppermute x5, starting transfers between devices, halo(): lax.ppermute(head, BOTH, downward)  6.63 us
  transfers between devices with their start and end apart: 14, of which 3 were waited for; matrix products, arithmetic and copies ran while one was open for 1% of the time, Pallas kernels for 15%

profile of v2, /device:TPU:0, one launch (start us, length us, event | category | flops | bytes accessed | tf_op | source)
XLA Modules:
  0.0 201.8 jit_solution(9600269916810847239)
XLA Ops:
  2.7 3.0 %collective-permute-start.2 = (f32[3,512]{1,0:T(4,128)S(1)}, f32[3,512]{1,0:T(4,128)S(1)}, u32[]{:S(2)}, u32[]{:S(2)}) collective-permute-start(f32[3,512]{1,0:T(4,128)S(1)} %get-tuple-element.101), channel_id=1, source_target_pairs={{0,1},{1,2},{2,3},{3,4},{4,5},{5,6},{6,7},{7,8},{8,9},{9,10},{10,1... | collective-permute-start | bytes 18440 | tf_op jit(solution)/shard_map/ppermute | solution.py:295
  7.9 5.1 %collective-permute-start = (f32[32,512]{1,0:T(8,128)S(1)}, f32[32,512]{1,0:T(8,128)S(1)}, u32[]{:S(2)}, u32[]{:S(2)}) collective-permute-start(f32[32,512]{1,0:T(8,128)S(1)} %get-tuple-element.99), channel_id=1, source_target_pairs={{0,1},{1,2},{2,3},{3,4},{4,5},{5,6},{6,7},{7,8},{8,9},{9,10},{10,1... | collective-permute-start | bytes 196616 | tf_op jit(solution)/shard_map/ppermute | solution.py:295
  13.0 3.1 %copy-done.18 = f32[7,128,2048]{2,1,0:T(8,128)S(1)} copy-done((f32[7,128,2048]{2,1,0:T(8,128)S(1)}, f32[7,128,2048]{2,1,0:T(8,128)}, u32[]{:S(2)}) %copy-start.18) | copy-done | bytes 7340056
  17.2 3.0 %shard_map.70 = (f32[32,384]{1,0:T(8,128)S(1)}, f32[32,8,128]{2,1,0:T(8,128)}) custom-call(f32[32,2048]{1,0:T(8,128)S(1)} %copy-done.19, bf16[896,2048]{1,0:T(8,128)(2,1)S(1)} %get-tuple-element.50.high_ref.refs_0_, bf16[896,2048]{1,0:T(8,128)(2,1)S(1)} %get-tuple-element.51.low_ref.refs_1_), custom_call_target="tpu_custom_call" | custom-call | bytes 1048576 | tf_op jit(solution)/shard_map/pallas_call | solution.py:61
  22.0 9.7 %all-to-all-start = ((f32[32,8,128]{2,1,0:T(8,128)}), f32[32,8,128]{2,1,0:T(8,128)S(1)}, u32[]{:S(2)}, u32[]{:S(2)}) async-start(f32[32,8,128]{2,1,0:T(8,128)} %get-tuple-element.56), calls=%async_computation | async-start | bytes 262144 | tf_op jit(solution)/shard_map/all_to_all | solution.py:298
  32.4 12.3 %shard_map.69 = (bf16[9,512,512]{2,1,0:T(8,128)(2,1)S(1)}, bf16[9,512,512]{2,1,0:T(8,128)(2,1)S(1)}) custom-call(f32[3,3072]{1,0:T(4,128)S(1)} %constant_dynamic-update-slice_fusion.lane_ref, f32[3072,3]{1,0:T(8,128)S(1)} %bitcast.3), custom_call_target="tpu_custom_call" | custom-call | bytes 1048576 | tf_op jit(solution)/shard_map/pallas_call | solution.py:61
  44.7 3.4 %shard_map.71 = (f32[32,2048]{1,0:T(8,128)S(1)}, f32[32,128]{1,0:T(8,128)S(1)}) custom-call(s32[1]{0:T(128)} %bitcast.refs_0_, s32[4,3]{1,0:T(4,128)S(1)} %copy-done.21, f32[32,2048]{1,0:T(8,128)S(1)} %copy-done.19, f32[32,512]{1,0:T(8,128)S(1)} %collective-permute-done.refs_3_, f32[32,512]{1,0:T(8,128)S(1)} %collective-permute-done.1.refs_4_, ...), custom_call_target="tpu_custom_call" | custom-call | flops 1610612736 | bytes 1048576 | tf_op jit(solution)/shard_map/pallas_call | solution.py:61
  52.8 13.9 %all_to_all.40.refs_4_ = f32[32,8,128]{2,1,0:T(8,128)S(1)} all-to-all(f32[32,8,128]{2,1,0:T(8,128)S(1)} %shard_map.72.refs_3_), channel_id=1, replica_groups=mesh['row'=8,'col'=4] {'row','col'}, dimensions={0} | all-to-all | bytes 262144 | tf_op jit(solution)/shard_map/all_to_all | solution.py:298
  72.1 3.0 %shard_map.74 = (f32[32,384]{1,0:T(8,128)S(1)}, f32[32,8,128]{2,1,0:T(8,128)}) custom-call(f32[32,2048]{1,0:T(8,128)S(1)} %get-tuple-element.58.field_ref.refs_2_.refs_3_, bf16[896,2048]{1,0:T(8,128)(2,1)S(1)} %copy-done.1, bf16[896,2048]{1,0:T(8,128)(2,1)S(1)} %copy-done.6), custom_call_target="tpu_custom_call" | custom-call | bytes 1048576 | tf_op jit(solution)/shard_map/pallas_call | solution.py:61
  75.1 2.6 %all-to-all-start.2 = ((f32[32,8,128]{2,1,0:T(8,128)}), f32[32,8,128]{2,1,0:T(8,128)S(1)}, u32[]{:S(2)}, u32[]{:S(2)}) async-start(f32[32,8,128]{2,1,0:T(8,128)} %get-tuple-element.66), calls=%async_computation.2 | async-start | bytes 262144 | tf_op jit(solution)/shard_map/all_to_all | solution.py:298
  81.1 3.0 %collective-permute-done.5.refs_4_ = f32[32,512]{1,0:T(8,128)S(1)} collective-permute-done((f32[32,512]{1,0:T(8,128)S(1)}, f32[32,512]{1,0:T(8,128)S(1)}, u32[]{:S(2)}, u32[]{:S(2)}) %collective-permute-start.5) | collective-permute-done | bytes 65568 | tf_op jit(solution)/shard_map/ppermute | solution.py:295
  84.1 2.3 %copy-done.11 = bf16[9,512,512]{2,1,0:T(8,128)(2,1)S(1)} copy-done((bf16[9,512,512]{2,1,0:T(8,128)(2,1)S(1)}, bf16[9,512,512]{2,1,0:T(8,128)(2,1)}, u32[]{:S(2)}) %copy-start.11) | copy-done | bytes 4718616
  88.7 3.5 %shard_map.75 = (f32[32,2048]{1,0:T(8,128)S(1)}, f32[32,128]{1,0:T(8,128)S(1)}) custom-call(s32[1]{0:T(128)} %bitcast.refs_0_, s32[4,3]{1,0:T(4,128)S(1)} %copy-done.21, f32[32,2048]{1,0:T(8,128)S(1)} %get-tuple-element.58.field_ref.refs_2_.refs_3_, f32[32,512]{1,0:T(8,128)S(1)} %collective-permute-done.4.refs_3_, ...), custom_call_target="tpu_custom_call" | custom-call | flops 1610612736 | bytes 1048576 | tf_op jit(solution)/shard_map/pallas_call | solution.py:61
  92.4 17.1 %all_to_all.41.refs_4_ = f32[32,8,128]{2,1,0:T(8,128)S(1)} all-to-all(f32[32,8,128]{2,1,0:T(8,128)S(1)} %get-tuple-element.68.refs_3_), channel_id=1, replica_groups=mesh['row'=8,'col'=4] {'row','col'}, dimensions={0} | all-to-all | bytes 262144 | tf_op jit(solution)/shard_map/all_to_all | solution.py:298
  115.0 3.0 %shard_map.78 = (f32[32,384]{1,0:T(8,128)S(1)}, f32[32,8,128]{2,1,0:T(8,128)}) custom-call(f32[32,2048]{1,0:T(8,128)S(1)} %get-tuple-element.71.field_ref.refs_2_.refs_3_, bf16[896,2048]{1,0:T(8,128)(2,1)S(1)} %copy-done.2, bf16[896,2048]{1,0:T(8,128)(2,1)S(1)} %copy-done.7), custom_call_target="tpu_custom_call" | custom-call | bytes 1048576 | tf_op jit(solution)/shard_map/pallas_call | solution.py:61
  118.0 2.6 %all-to-all-start.4 = ((f32[32,8,128]{2,1,0:T(8,128)}), f32[32,8,128]{2,1,0:T(8,128)S(1)}, u32[]{:S(2)}, u32[]{:S(2)}) async-start(f32[32,8,128]{2,1,0:T(8,128)} %get-tuple-element.79), calls=%async_computation.4 | async-start | bytes 262144 | tf_op jit(solution)/shard_map/all_to_all | solution.py:298
  124.1 2.8 %collective-permute-done.7.refs_4_ = f32[32,512]{1,0:T(8,128)S(1)} collective-permute-done((f32[32,512]{1,0:T(8,128)S(1)}, f32[32,512]{1,0:T(8,128)S(1)}, u32[]{:S(2)}, u32[]{:S(2)}) %collective-permute-start.7) | collective-permute-done | bytes 65568 | tf_op jit(solution)/shard_map/ppermute | solution.py:295
  131.6 3.5 %shard_map.79 = (f32[32,2048]{1,0:T(8,128)S(1)}, f32[32,128]{1,0:T(8,128)S(1)}) custom-call(s32[1]{0:T(128)} %bitcast.refs_0_, s32[4,3]{1,0:T(4,128)S(1)} %copy-done.21, f32[32,2048]{1,0:T(8,128)S(1)} %get-tuple-element.71.field_ref.refs_2_.refs_3_, f32[32,512]{1,0:T(8,128)S(1)} %collective-permute-done.6.refs_3_, ...), custom_call_target="tpu_custom_call" | custom-call | flops 1610612736 | bytes 1048576 | tf_op jit(solution)/shard_map/pallas_call | solution.py:61
  135.5 17.1 %all_to_all.42.refs_4_ = f32[32,8,128]{2,1,0:T(8,128)S(1)} all-to-all(f32[32,8,128]{2,1,0:T(8,128)S(1)} %get-tuple-element.83.refs_3_), channel_id=1, replica_groups=mesh['row'=8,'col'=4] {'row','col'}, dimensions={0} | all-to-all | bytes 262144 | tf_op jit(solution)/shard_map/all_to_all | solution.py:298
  158.1 3.0 %shard_map.82 = (f32[32,384]{1,0:T(8,128)S(1)}, f32[32,8,128]{2,1,0:T(8,128)}) custom-call(f32[32,2048]{1,0:T(8,128)S(1)} %get-tuple-element.85.field_ref.refs_2_.refs_3_, bf16[896,2048]{1,0:T(8,128)(2,1)S(1)} %copy-done.3, bf16[896,2048]{1,0:T(8,128)(2,1)S(1)} %copy-done.8), custom_call_target="tpu_custom_call" | custom-call | bytes 1048576 | tf_op jit(solution)/shard_map/pallas_call | solution.py:61
  161.1 2.6 %all-to-all-start.6 = ((f32[32,8,128]{2,1,0:T(8,128)}), f32[32,8,128]{2,1,0:T(8,128)S(1)}, u32[]{:S(2)}, u32[]{:S(2)}) async-start(f32[32,8,128]{2,1,0:T(8,128)} %get-tuple-element.93), calls=%async_computation.6 | async-start | bytes 262144 | tf_op jit(solution)/shard_map/all_to_all | solution.py:298
  167.0 3.0 %collective-permute-done.9.refs_4_ = f32[32,512]{1,0:T(8,128)S(1)} collective-permute-done((f32[32,512]{1,0:T(8,128)S(1)}, f32[32,512]{1,0:T(8,128)S(1)}, u32[]{:S(2)}, u32[]{:S(2)}) %collective-permute-start.9) | collective-permute-done | bytes 65568 | tf_op jit(solution)/shard_map/ppermute | solution.py:295
  174.6 3.5 %shard_map.83 = (f32[32,2048]{1,0:T(8,128)S(1)}, f32[32,128]{1,0:T(8,128)S(1)}) custom-call(s32[1]{0:T(128)} %bitcast.refs_0_, s32[4,3]{1,0:T(4,128)S(1)} %copy-done.21, f32[32,2048]{1,0:T(8,128)S(1)} %get-tuple-element.85.field_ref.refs_2_.refs_3_, f32[32,512]{1,0:T(8,128)S(1)} %collective-permute-done.8.refs_3_, ...), custom_call_target="tpu_custom_call" | custom-call | flops 1610612736 | bytes 1048576 | tf_op jit(solution)/shard_map/pallas_call | solution.py:61
  178.5 17.1 %all_to_all.43.refs_4_ = f32[32,8,128]{2,1,0:T(8,128)S(1)} all-to-all(f32[32,8,128]{2,1,0:T(8,128)S(1)} %shard_map.84), channel_id=1, replica_groups=mesh['row'=8,'col'=4] {'row','col'}, dimensions={0} | all-to-all | bytes 262144 | tf_op jit(solution)/shard_map/all_to_all | solution.py:298
  (78 shorter events, 57.7 us)
Async XLA Ops:
  0.6 16.6 %copy-start.19 = (f32[32,2048]{1,0:T(8,128)S(1)}, f32[32,2048]{1,0:T(8,128)}, u32[]{:S(2)}) copy-start(f32[32,2048]{1,0:T(8,128)} %refs_3_.1) | copy-start | bytes 786436
  1.4 30.4 %collective-permute-start.3 = (f32[3,512]{1,0:T(4,128)S(1)}, f32[3,512]{1,0:T(4,128)S(1)}, u32[]{:S(2)}, u32[]{:S(2)}) collective-permute-start(f32[3,512]{1,0:T(4,128)S(1)} %get-tuple-element.100), channel_id=1, source_target_pairs={{1,0},{2,1},{3,2},{4,3},{5,4},{6,5},{7,6},{8,7},{9,8},{10,9},{11,1... | collective-permute-start | bytes 18440 | tf_op jit(solution)/shard_map/ppermute | solution.py:295
  2.7 29.1 %collective-permute-start.2 = (f32[3,512]{1,0:T(4,128)S(1)}, f32[3,512]{1,0:T(4,128)S(1)}, u32[]{:S(2)}, u32[]{:S(2)}) collective-permute-start(f32[3,512]{1,0:T(4,128)S(1)} %get-tuple-element.101), channel_id=1, source_target_pairs={{0,1},{1,2},{2,3},{3,4},{4,5},{5,6},{6,7},{7,8},{8,9},{9,10},{10,1... | collective-permute-start | bytes 18440 | tf_op jit(solution)/shard_map/ppermute | solution.py:295
  6.6 38.1 %collective-permute-start.1 = (f32[32,512]{1,0:T(8,128)S(1)}, f32[32,512]{1,0:T(8,128)S(1)}, u32[]{:S(2)}, u32[]{:S(2)}) collective-permute-start(f32[32,512]{1,0:T(8,128)S(1)} %get-tuple-element.98), channel_id=1, source_target_pairs={{1,0},{2,1},{3,2},{4,3},{5,4},{6,5},{7,6},{8,7},{9,8},{10,9},{11,1... | collective-permute-start | bytes 196616 | tf_op jit(solution)/shard_map/ppermute | solution.py:295
  7.9 36.8 %collective-permute-start = (f32[32,512]{1,0:T(8,128)S(1)}, f32[32,512]{1,0:T(8,128)S(1)}, u32[]{:S(2)}, u32[]{:S(2)}) collective-permute-start(f32[32,512]{1,0:T(8,128)S(1)} %get-tuple-element.99), channel_id=1, source_target_pairs={{0,1},{1,2},{2,3},{3,4},{4,5},{5,6},{6,7},{7,8},{8,9},{9,10},{10,1... | collective-permute-start | bytes 196616 | tf_op jit(solution)/shard_map/ppermute | solution.py:295
  13.0 3.1 %copy-start.18 = (f32[7,128,2048]{2,1,0:T(8,128)S(1)}, f32[7,128,2048]{2,1,0:T(8,128)}, u32[]{:S(2)}) copy-start(f32[7,128,2048]{2,1,0:T(8,128)} %basis_ref.1) | copy-start | bytes 22020100
  17.2 3.1 %copy-start.5 = (bf16[896,2048]{1,0:T(8,128)(2,1)}, bf16[896,2048]{1,0:T(8,128)(2,1)S(1)}, u32[]{:S(2)}) copy-start(bf16[896,2048]{1,0:T(8,128)(2,1)S(1)} %get-tuple-element.51.low_ref.refs_1_) | copy-start | bytes 11010052
  17.2 14.6 %copy-start.22 = (f32[3,2048]{1,0:T(4,128)S(1)}, f32[3,2048]{1,0:T(4,128)}, u32[]{:S(2)}) copy-start(f32[3,2048]{1,0:T(4,128)} %param.6) | copy-start | bytes 73732
  17.2 27.5 %copy-start.20 = (f32[2048]{0:T(1024)S(1)}, f32[2048]{0:T(1024)}, u32[]{:S(2)}) copy-start(f32[2048]{0:T(1024)} %param.7) | copy-start | bytes 24580
  17.2 27.5 %copy-start.21 = (s32[4,3]{1,0:T(4,128)S(1)}, s32[4,3]{1,0:T(4,128)}, u32[]{:S(2)}) copy-start(s32[4,3]{1,0:T(4,128)} %refs_1_.7) | copy-start | bytes 148
  22.0 30.5 %all-to-all-start = ((f32[32,8,128]{2,1,0:T(8,128)}), f32[32,8,128]{2,1,0:T(8,128)S(1)}, u32[]{:S(2)}, u32[]{:S(2)}) async-start(f32[32,8,128]{2,1,0:T(8,128)} %get-tuple-element.56), calls=%async_computation | async-start | bytes 262144 | tf_op jit(solution)/shard_map/all_to_all | solution.py:298
  75.1 17.0 %all-to-all-start.2 = ((f32[32,8,128]{2,1,0:T(8,128)}), f32[32,8,128]{2,1,0:T(8,128)S(1)}, u32[]{:S(2)}, u32[]{:S(2)}) async-start(f32[32,8,128]{2,1,0:T(8,128)} %get-tuple-element.66), calls=%async_computation.2 | async-start | bytes 262144 | tf_op jit(solution)/shard_map/all_to_all | solution.py:298
  77.7 3.3 %collective-permute-start.4 = (f32[32,512]{1,0:T(8,128)S(1)}, f32[32,512]{1,0:T(8,128)S(1)}, u32[]{:S(2)}, u32[]{:S(2)}) collective-permute-start(f32[32,512]{1,0:T(8,128)S(1)} %get-tuple-element.59), channel_id=1, source_target_pairs={{0,1},{1,2},{2,3},{3,4},{4,5},{5,6},{6,7},{7,8},{8,9},{9,10},{10,1... | collective-permute-start | bytes 196616 | tf_op jit(solution)/shard_map/ppermute | solution.py:295
  79.8 4.3 %collective-permute-start.5 = (f32[32,512]{1,0:T(8,128)S(1)}, f32[32,512]{1,0:T(8,128)S(1)}, u32[]{:S(2)}, u32[]{:S(2)}) collective-permute-start(f32[32,512]{1,0:T(8,128)S(1)} %get-tuple-element.60), channel_id=1, source_target_pairs={{1,0},{2,1},{3,2},{4,3},{5,4},{6,5},{7,6},{8,7},{9,8},{10,9},{11,1... | collective-permute-start | bytes 196616 | tf_op jit(solution)/shard_map/ppermute | solution.py:295
  84.1 2.3 %copy-start.11 = (bf16[9,512,512]{2,1,0:T(8,128)(2,1)S(1)}, bf16[9,512,512]{2,1,0:T(8,128)(2,1)}, u32[]{:S(2)}) copy-start(bf16[9,512,512]{2,1,0:T(8,128)(2,1)} %copy-done.10) | copy-start | bytes 14155780
  86.4 2.3 %copy-start.15 = (bf16[9,512,512]{2,1,0:T(8,128)(2,1)S(1)}, bf16[9,512,512]{2,1,0:T(8,128)(2,1)}, u32[]{:S(2)}) copy-start(bf16[9,512,512]{2,1,0:T(8,128)(2,1)} %copy-done.14) | copy-start | bytes 14155780
  118.0 17.0 %all-to-all-start.4 = ((f32[32,8,128]{2,1,0:T(8,128)}), f32[32,8,128]{2,1,0:T(8,128)S(1)}, u32[]{:S(2)}, u32[]{:S(2)}) async-start(f32[32,8,128]{2,1,0:T(8,128)} %get-tuple-element.79), calls=%async_computation.4 | async-start | bytes 262144 | tf_op jit(solution)/shard_map/all_to_all | solution.py:298
  120.6 3.5 %collective-permute-start.6 = (f32[32,512]{1,0:T(8,128)S(1)}, f32[32,512]{1,0:T(8,128)S(1)}, u32[]{:S(2)}, u32[]{:S(2)}) collective-permute-start(f32[32,512]{1,0:T(8,128)S(1)} %get-tuple-element.72), channel_id=1, source_target_pairs={{0,1},{1,2},{2,3},{3,4},{4,5},{5,6},{6,7},{7,8},{8,9},{9,10},{10,1... | collective-permute-start | bytes 196616 | tf_op jit(solution)/shard_map/ppermute | solution.py:295
  122.7 4.3 %collective-permute-start.7 = (f32[32,512]{1,0:T(8,128)S(1)}, f32[32,512]{1,0:T(8,128)S(1)}, u32[]{:S(2)}, u32[]{:S(2)}) collective-permute-start(f32[32,512]{1,0:T(8,128)S(1)} %get-tuple-element.73), channel_id=1, source_target_pairs={{1,0},{2,1},{3,2},{4,3},{5,4},{6,5},{7,6},{8,7},{9,8},{10,9},{11,1... | collective-permute-start | bytes 196616 | tf_op jit(solution)/shard_map/ppermute | solution.py:295
  126.9 2.3 %copy-start.12 = (bf16[9,512,512]{2,1,0:T(8,128)(2,1)S(1)}, bf16[9,512,512]{2,1,0:T(8,128)(2,1)}, u32[]{:S(2)}) copy-start(bf16[9,512,512]{2,1,0:T(8,128)(2,1)} %copy-done.10) | copy-start | bytes 14155780
  161.1 17.0 %all-to-all-start.6 = ((f32[32,8,128]{2,1,0:T(8,128)}), f32[32,8,128]{2,1,0:T(8,128)S(1)}, u32[]{:S(2)}, u32[]{:S(2)}) async-start(f32[32,8,128]{2,1,0:T(8,128)} %get-tuple-element.93), calls=%async_computation.6 | async-start | bytes 262144 | tf_op jit(solution)/shard_map/all_to_all | solution.py:298
  163.7 3.3 %collective-permute-start.8 = (f32[32,512]{1,0:T(8,128)S(1)}, f32[32,512]{1,0:T(8,128)S(1)}, u32[]{:S(2)}, u32[]{:S(2)}) collective-permute-start(f32[32,512]{1,0:T(8,128)S(1)} %get-tuple-element.86), channel_id=1, source_target_pairs={{0,1},{1,2},{2,3},{3,4},{4,5},{5,6},{6,7},{7,8},{8,9},{9,10},{10,1... | collective-permute-start | bytes 196616 | tf_op jit(solution)/shard_map/ppermute | solution.py:295
  165.7 4.3 %collective-permute-start.9 = (f32[32,512]{1,0:T(8,128)S(1)}, f32[32,512]{1,0:T(8,128)S(1)}, u32[]{:S(2)}, u32[]{:S(2)}) collective-permute-start(f32[32,512]{1,0:T(8,128)S(1)} %get-tuple-element.87), channel_id=1, source_target_pairs={{1,0},{2,1},{3,2},{4,3},{5,4},{6,5},{7,6},{8,7},{9,8},{10,9},{11,1... | collective-permute-start | bytes 196616 | tf_op jit(solution)/shard_map/ppermute | solution.py:295
  170.0 2.3 %copy-start.13 = (bf16[9,512,512]{2,1,0:T(8,128)(2,1)S(1)}, bf16[9,512,512]{2,1,0:T(8,128)(2,1)}, u32[]{:S(2)}) copy-start(bf16[9,512,512]{2,1,0:T(8,128)(2,1)} %copy-done.10) | copy-start | bytes 14155780
  (13 other events, 27.1 us)
